TPU v7x, 32 devices: a whole 2x2x4 slice. The times are simulated.
32 devices in a mesh: row: 8 (over y, x, core), col: 4 (over z).
Axes of the slice: x: 2, y: 2, z: 4, core: 2. Of those that a mesh axis runs over, the one named last changes fastest.
Arguments:
- vectors_in: float32 [4096, 1024], P('row', 'col'), may hold values from -6 to 6
- poles_one: float32 [2, 2048], replicated, may hold values from 0 to 2048, as said below
- roots_one: float32 [2, 2048], replicated, may hold values from 0 to 2048, as said below
- order_one: int32 [2, 2048], replicated, may hold values from 0 to 2047, each once within a row
- deflate_one: int32 [2, 2048], replicated, may hold values 0 or 1
- poles_two: float32 [4096], replicated, may hold values from 0 to 4096, as said below
- roots_two: float32 [4096], replicated, may hold values from 0 to 4096, as said below
- order_two: int32 [4096], replicated, may hold values from 0 to 4095, each once
- deflate_two: int32 [4096], replicated, may hold values 0 or 1
Outputs:
- merged: float32 [4096, 4096], P('row', 'col')
Inputs may be any that keep to these rules, and one draw needn't show every extreme that they name: `poles_one`: along the last dimension, the entry at position k lies between k and k + 0.3. `roots_one`: along the last dimension, the entry at position k lies between k + 0.45 and k + 0.75. `poles_two`: the entry at position k lies between k and k + 0.3. `roots_two`: the entry at position k lies between k + 0.45 and k + 0.75.
All inputs are finite; a program needn't handle non-finite values.
Results may differ from a plain program's by a relative error of at most 0.0003.
Values sent between devices are 32-bit elements; how exact they have to be, the bound alone decides.
No kernel may reach another device: no remote copies, remote signals or barrier semaphores. Data moves between devices by JAX's collectives and lax.ppermute only.
A program may use at most 64 MiB of HBM per device.

v0:
```python
import math

import jax
import jax.numpy as jnp
from jax import lax
from jax.sharding import PartitionSpec as P


def setup_level(z_full, pole_vals, root_vals, order_vals, deflate, col_first, col_span):
    level_size = pole_vals.shape[0]
    inverse = jnp.argsort(order_vals)
    kept_mask = (1 - deflate).astype(jnp.float32)
    deflated = deflate.astype(jnp.float32)
    targets = col_first + jnp.arange(col_span, dtype=jnp.int32)
    root_cols = lax.dynamic_slice_in_dim(root_vals, col_first, col_span)
    dropped = lax.dynamic_slice_in_dim(deflated, col_first, col_span)
    stride = math.gcd(level_size, 128)

    def add_squares(block_step, running):
        first_row = block_step * stride
        inv_rows = lax.dynamic_slice_in_dim(inverse, first_row, stride)
        z_rows = lax.dynamic_slice_in_dim(z_full, first_row, stride)
        cauchy = z_rows[:, None] / (jnp.take(pole_vals, inv_rows)[:, None] - root_cols[None, :])
        return running + jnp.sum(jnp.take(kept_mask, inv_rows)[:, None] * cauchy * cauchy, axis=0)

    squares = lax.fori_loop(
        0, level_size // stride, add_squares, jnp.zeros((col_span,), jnp.float32)
    )
    scales = lax.rsqrt(squares + 1e-06)
    return (z_full, pole_vals, inverse, kept_mask, root_cols, dropped, targets, scales)


def coef_rows(context, row_first, row_span):
    z_full, pole_vals, inverse, kept_mask, root_cols, dropped, targets, scales = context
    inv_rows = lax.dynamic_slice_in_dim(inverse, row_first, row_span)
    z_rows = lax.dynamic_slice_in_dim(z_full, row_first, row_span)
    cauchy = z_rows[:, None] / (jnp.take(pole_vals, inv_rows)[:, None] - root_cols[None, :])
    matches = (inv_rows[:, None] == targets[None, :]).astype(jnp.float32)
    kept_rows = jnp.take(kept_mask, inv_rows)
    return (
        kept_rows[:, None] * (1.0 - dropped)[None, :] * cauchy * scales[None, :]
        + dropped[None, :] * matches
    )


def apply_rows(summed, columns, offset, context):
    span_cols = columns.shape[1]
    stride = math.gcd(span_cols, 128)

    def add_block(block_step, running):
        begin_col = block_step * stride
        part_cols = lax.dynamic_slice_in_dim(columns, begin_col, stride, 1)
        factors = coef_rows(context, offset + begin_col, stride)
        return running + jnp.dot(
            part_cols, factors, precision=lax.Precision.HIGHEST, preferred_element_type=jnp.float32
        )

    return lax.fori_loop(0, span_cols // stride, add_block, summed)


def body(
    vectors_in,
    poles_one,
    roots_one,
    order_one,
    deflate_one,
    poles_two,
    roots_two,
    order_two,
    deflate_two,
):
    row_total = lax.axis_size("row")
    col_total = lax.axis_size("col")
    row_place = lax.axis_index("row")
    col_place = lax.axis_index("col")
    local_rows, leaf_share = vectors_in.shape
    leaf_width = leaf_share * col_total
    per_leaf = row_total // 4
    leaf_number = row_place // per_leaf
    pair_number = leaf_number // 2
    side_number = leaf_number % 2

    def choose_pair(table):
        return lax.dynamic_index_in_dim(table, pair_number, 0, keepdims=False)

    edge_vec = jnp.where(side_number == 0, vectors_in[-1], vectors_in[0])
    at_edge = jnp.where(
        side_number == 0, row_place % per_leaf == per_leaf - 1, row_place % per_leaf == 0
    ).astype(jnp.float32)
    pair_slot = (jnp.arange(2) == pair_number).astype(jnp.float32)
    side_slot = (jnp.arange(2) == side_number).astype(jnp.float32)
    edge_part = (pair_slot[:, None] * side_slot[None, :])[:, :, None] * (at_edge * edge_vec)[
        None, None, :
    ]
    row_summed = lax.psum(edge_part, "row")
    edges_one = lax.all_gather(row_summed, "col", axis=2, tiled=True)
    z_one = choose_pair(edges_one).reshape(2 * leaf_width)
    width_one = 2 * leaf_width
    share_one = width_one // col_total
    first_one = col_place * share_one
    context_one = setup_level(
        z_one,
        choose_pair(poles_one),
        choose_pair(roots_one),
        choose_pair(order_one),
        choose_pair(deflate_one),
        first_one,
        share_one,
    )
    offset_one = side_number * leaf_width
    level_one = apply_rows(
        jnp.zeros((local_rows, share_one), jnp.float32),
        lax.all_gather(vectors_in, "col", axis=1, tiled=True),
        offset_one,
        context_one,
    )
    half_rows = row_total // 2
    half_number = row_place // half_rows
    edge_two = jnp.where(half_number == 0, level_one[-1], level_one[0])
    at_two = ((row_place == half_rows - 1) | (row_place == half_rows)).astype(jnp.float32)
    half_slot = (jnp.arange(2) == half_number).astype(jnp.float32)
    part_two = half_slot[:, None] * (at_two * edge_two)[None, :]
    rows_two = lax.psum(part_two, "row")
    edges_two = lax.all_gather(rows_two, "col", axis=1, tiled=True)
    z_two = edges_two.reshape(2 * width_one)
    width_two = 2 * width_one
    share_two = width_two // col_total
    context_two = setup_level(
        z_two, poles_two, roots_two, order_two, deflate_two, col_place * share_two, share_two
    )
    offset_two = half_number * width_one
    empty_two = jnp.zeros((local_rows, share_two), jnp.float32)
    return apply_rows(
        empty_two, lax.all_gather(level_one, "col", axis=1, tiled=True), offset_two, context_two
    )


def solution(mesh):
    placed = (P("row", "col"), P(), P(), P(), P(), P(), P(), P(), P())
    return jax.shard_map(
        body, mesh=mesh, in_specs=placed, out_specs=P("row", "col"), check_vma=False
    )
```

profile of v0, /device:TPU:0, one launch (start us, length us, event | category | flops | bytes accessed | tf_op | source)
XLA Modules:
  0.0 351.2 jit_solution(7688537214055966694)
XLA Ops:
  8.3 15.1 %psum.14 = f32[2,2,256]{2,1,0:T(2,128)S(1)} all-reduce(f32[2,2,256]{2,1,0:T(2,128)S(1)} %broadcast_multiply_fusion.1), channel_id=1, replica_groups=mesh['row'=8,'col'=4] {'row'}, use_global_device_ids=true, to_apply=%region_1.2 | all-reduce | flops 1024 | bytes 8192 | tf_op jit(solution)/shard_map/psum | solution.py:95
  24.9 12.8 %all_gather.13 = f32[2,2,1024]{2,1,0:T(2,128)S(1)} all-gather(f32[2,2,256]{2,1,0:T(2,128)S(1)} %psum.14), channel_id=1, replica_groups=mesh['row'=8,'col'=4] {'col'}, dimensions={2}, use_global_device_ids=true | all-gather | bytes 20480 | tf_op jit(solution)/shard_map/all_gather | solution.py:96
  37.7 5.0 %sort.34 = (s32[2048]{0:T(1024)}, s32[2048]{0:T(1024)S(1)}) sort(s32[2048]{0:T(1024)S(1)} %bitcast.19, s32[2048]{0:T(1024)S(1)} %iota.29), dimensions={0}, to_apply=%region_0.1 | sort | flops 22528 | bytes 32768 | tf_op jit(solution)/shard_map/jit(argsort)/sort | solution.py:11
  43.5 43.8 %while.56 = (s32[]{:T(128)}, f32[512]{0:T(512)S(1)}, s32[2048]{0:T(1024)S(1)}, f32[2048]{0:T(1024)S(1)}, f32[2048]{0:T(1024)S(1)}, /*index=5*/f32[2048]{0:T(1024...) while((s32[]{:T(128)}, f32[512]{0:T(512)S(1)}, ...), condition=%wide.region_4.6_spmd.clone, body=%wide.region_2.5_spmd.clone.sunk | while | flops 330631 | bytes 24249 | solution.py:26
  87.3 5.8 %sort.35 = (s32[4096]{0:T(1024)}, s32[4096]{0:T(1024)S(1)}) sort(s32[4096]{0:T(1024)S(1)} %copy-done.5, s32[4096]{0:T(1024)S(1)} %iota.33), dimensions={0}, to_apply=%region_7.9 | sort | flops 49152 | bytes 65536 | tf_op jit(solution)/shard_map/jit(argsort)/sort | solution.py:11
  93.9 38.2 %while.57 = (s32[]{:T(128)}, f32[512,512]{1,0:T(8,128)S(1)}, f32[512,1024]{1,0:T(8,128)}, s32[]{:T(128)}, s32[2048]{0:T(1024)S(1)}, /*index=5*/f32[2048]{0:T(102...) while((s32[]{:T(128)}, f32[512,512]{1,0:T(8,128)S(1)}, ...), condition=%wide.region_6.8_spmd.clone, body=%wide.region_5.7_spmd.clone.sunk | while | flops 403705216 | bytes 2390811 | solution.py:58
  133.9 11.8 %psum.15 = f32[2,512]{1,0:T(2,128)S(1)} all-reduce(f32[2,512]{1,0:T(2,128)S(1)} %broadcast_multiply_fusion), channel_id=1, replica_groups=mesh['row'=8,'col'=4] {'row'}, use_global_device_ids=true, to_apply=%region_8.10 | all-reduce | flops 1024 | bytes 8192 | tf_op jit(solution)/shard_map/psum | solution.py:123
  145.7 13.3 %all_gather.15 = f32[2,2048]{1,0:T(2,128)S(1)} all-gather(f32[2,512]{1,0:T(2,128)S(1)} %psum.15), channel_id=1, replica_groups=mesh['row'=8,'col'=4] {'col'}, dimensions={1}, use_global_device_ids=true | all-gather | bytes 20480 | tf_op jit(solution)/shard_map/all_gather | solution.py:124
  159.0 89.2 %while.58 = (s32[]{:T(128)}, f32[1024]{0:T(1024)S(1)}, s32[4096]{0:T(1024)S(1)}, f32[4096]{0:T(1024)S(1)}, f32[4096]{0:T(1024)S(1)}, /*index=5*/f32[4096]{0:T(10...) while((s32[]{:T(128)}, f32[1024]{0:T(1024)S(1)}, ...), condition=%wide.region_11.14_spmd.clone, body=%wide.region_9.13_spmd.clone.sunk | while | flops 658823 | bytes 34489 | solution.py:26
  248.3 94.7 %while.59 = (s32[]{:T(128)}, f32[512,1024]{1,0:T(8,128)S(1)}, f32[512,2048]{1,0:T(8,128)}, s32[]{:T(128)}, s32[4096]{0:T(1024)S(1)}, /*index=5*/f32[4096]{0:T(10...) while((s32[]{:T(128)}, f32[512,1024]{1,0:T(8,128)S(1)}, ...), condition=%wide.region_13.16_spmd.clone, body=%wide.region_12.15_spmd.clone.sunk | while | flops 807408000 | bytes 4504347 | solution.py:58
  256.7 3.4 select_add_fusion.8
  262.6 3.4 select_add_fusion.8
  268.6 3.4 select_add_fusion.8
  274.5 3.4 select_add_fusion.8
  280.4 3.4 select_add_fusion.8
  286.3 3.4 select_add_fusion.8
  292.2 3.4 select_add_fusion.8
  298.2 3.4 select_add_fusion.8
  304.1 3.4 select_add_fusion.8
  310.0 3.4 select_add_fusion.8
  315.9 3.4 select_add_fusion.8
  321.8 3.4 select_add_fusion.8
  327.8 3.4 select_add_fusion.8
  339.6 3.4 select_add_fusion.8
  (631 shorter events, 222.2 us)
Async XLA Ops:
  6.5 16.8 %copy-start = (f32[2,2048]{1,0:T(2,128)S(1)}, f32[2,2048]{1,0:T(2,128)}, u32[]{:S(2)}) copy-start(f32[2,2048]{1,0:T(2,128)} %param.22) | copy-start | bytes 49156
  6.5 87.4 %all-gather.3.cloned.1.call-start = ((), (), s32[]{:S(2)}) async-start(), calls=%async_computation | async-start | bytes 2621440 | tf_op jit(solution)/shard_map/all_gather | solution.py:113
  7.3 241.0 %all-gather.5.cloned.1.call-start = ((), (), s32[]{:S(2)}) async-start(), calls=%async_computation.1 | async-start | bytes 5242880 | tf_op jit(solution)/shard_map/all_gather | solution.py:134
  43.5 43.8 %copy-start.5 = (s32[4096]{0:T(1024)S(1)}, s32[4096]{0:T(1024)}, u32[]{:S(2)}) copy-start(s32[4096]{0:T(1024)} %param.28) | copy-start | bytes 49156
  43.5 50.4 %copy-start.4 = (s32[4096]{0:T(1024)S(1)}, s32[4096]{0:T(1024)}, u32[]{:S(2)}) copy-start(s32[4096]{0:T(1024)} %param.29) | copy-start | bytes 49156
  93.9 65.1 %copy-start.1 = (f32[4096]{0:T(1024)S(1)}, f32[4096]{0:T(1024)}, u32[]{:S(2)}) copy-start(f32[4096]{0:T(1024)} %param.26) | copy-start | bytes 49156
  93.9 65.1 %dynamic-slice-start = ((f32[4096]{0:T(1024)}, s32[]{:T(128)}), f32[1024]{0:T(1024)S(1)}, s32[]{:S(2)}) async-start(f32[4096]{0:T(1024)} %param.27, s32[]{:T(128)} %select_n.142), calls=%async_computation.2 | async-start | bytes 8704 | tf_op jit(solution)/shard_map/dynamic_slice | solution.py:15
  132.1 1.0 copy-start.3
  343.0 1.3 copy-start.2
Sparse Core Ops, SparseCore 0:
  8.9 48.8 all-gather.2
  133.2 78.8 all-gather.4
where the time goes:
time: 352 us; the launch traced here: 351 us
  local copies, waits for them, and re-layouts  175 us (50%)
  matrix products  71.8 us (20%)
  blocking collectives  53 us (15%)
  other arithmetic  32.9 us (9%)
  between operations  13.7 us (4%)
  loops' own time  4.26 us (1%)
    dot_general x24, matrix products, add_block(): jnp.dot(part_cols, factors, precision=lax.Precision.HIGHEST, preferred_el...  71.8 us
    gather x48, local copies, waits for them, and re-layouts, add_squares(): jnp.take(kept_mask, inv_rows)[:, None] * cauchy * cauchy  55.1 us
    gather x48, local copies, waits for them, and re-layouts, add_squares(): jnp.take(pole_vals, inv_rows)[:, None] - root_cols[None, :]  55 us
    gather x24, local copies, waits for them, and re-layouts, coef_rows(): kept_rows = jnp.take(kept_mask, inv_rows)  27.6 us
    gather x24, local copies, waits for them, and re-layouts, coef_rows(): jnp.take(pole_vals, inv_rows)[:, None] - root_cols[None, :]  27.5 us
    psum x1, blocking collectives, body(): row_summed = lax.psum(edge_part, 'row')  15.1 us
    all_gather x1, blocking collectives, body(): edges_two = lax.all_gather(rows_two, 'col', axis=1, tiled=True)  13.3 us
    all_gather x1, blocking collectives, body(): edges_one = lax.all_gather(row_summed, 'col', axis=2, tiled=True)  12.8 us
  transfers between devices with their start and end apart: 2, of which 0 were waited for; matrix products, arithmetic and copies ran while one was open for 42% of the time, Pallas kernels for 0%

commit v1 on v0

v1 whole, which is shorter than its diff:
```python
import functools
import math

import jax
import jax.numpy as jnp
from jax import lax
from jax.experimental import pallas as pl
from jax.experimental.pallas import tpu as pltpu
from jax.sharding import PartitionSpec as P

F32 = jnp.float32
BF16 = jnp.bfloat16
LANES = 128
SOME_VMEM = 14 * 1024 * 1024
ROWS, WIDTH = 32, 512


def split(x):
    high = x.astype(BF16)
    return high, (x - high.astype(F32)).astype(BF16)


def dot3(a_high, a_low, b_high, b_low):
    dot = functools.partial(jnp.dot, preferred_element_type=F32)
    return dot(a_high, b_high) + dot(a_low, b_high) + dot(a_high, b_low)


def as_columns(row):
    count = row.shape[1] // LANES
    stacked = jnp.concatenate([row[:, LANES * b : LANES * (b + 1)] for b in range(count)], axis=0)
    return stacked.T


def permuted(order, low_bits, wanted, values):
    at_high = order >> 7 == wanted
    at_low = ((order & 127) == low_bits).astype(BF16)
    rows = jnp.concatenate([jnp.where(at_high, v, 0.0).astype(BF16) for v in values], axis=0)
    out = lax.dot_general(rows, at_low, (((1,), (1,)), ((), ())), preferred_element_type=F32)
    count = wanted.shape[0]
    return [out[count * i : count * (i + 1)] for i in range(len(values))]


def place_tables(order, poles, flags, wanted):
    span = order.shape[1]
    low_bits = lax.broadcasted_iota(jnp.int32, (LANES, span), 0)
    index = lax.broadcasted_iota(jnp.int32, (1, span), 1)
    first = poles.astype(BF16).astype(F32)
    second = (poles - first).astype(BF16).astype(F32)
    third = poles - first - second
    values = [first, second, third, (index >> 6).astype(F32), (index & 63).astype(F32), flags.astype(F32)]
    one, two, three, upper, lower, flag = permuted(order, low_bits, wanted, values)
    gone = flag > 0.5
    pole = jnp.where(gone, jnp.inf, one + two + three)
    target = jnp.where(gone, upper * 64.0 + lower, -1.0)
    return pole, target


def perm_kernel(place, order_one, poles_one, flags_one, order_two, poles_two, flags_two, one_out, two_out):
    pair, side, piece = place[0], place[1], place[2]
    blocks = 2 * place_blocks(order_one)
    spot = lax.broadcasted_iota(jnp.int32, (blocks, 1), 0)
    half = blocks // 2
    per = half // 4
    wanted_one = jnp.where(spot >= half, 1 - side, side) * half + (((spot % half) // per) ^ piece) * per + spot % per
    at = pl.ds(pair, 1)
    pole, target = place_tables(order_one[at, :], poles_one[at, :], flags_one[at, :], wanted_one)
    one_out[...] = jnp.concatenate([pole, target], axis=0).T
    pole, target = place_tables(order_two[...], poles_two[...], flags_two[...], spot + pair * blocks)
    two_out[...] = jnp.concatenate([pole, target], axis=0).T


def place_blocks(order_one):
    return order_one.shape[1] // (2 * LANES)


def kept_roots(roots, flags):
    return jnp.where(flags > 0, -jnp.inf, roots)


def inverse_gap(pole, target, roots, index):
    gap = pltpu.reciprocal(pole - roots, approx=True)
    return jnp.where(target == index, 1.0, gap)


def over_tiles(height, width, tile):
    for first in range(0, width, WIDTH):
        lanes = slice(first, first + WIDTH)
        for b in range(height // LANES):

            def step(i, _, b=b, lanes=lanes):
                near = pl.multiple_of(i * ROWS, ROWS)
                tile(b, pl.ds(near, ROWS), pl.ds(pl.multiple_of(b * LANES + near, ROWS), ROWS), lanes)
                return 0

            lax.fori_loop(0, LANES // ROWS, step, 0, unroll=LANES // ROWS)


def table_one_kernel(place, cols_ref, roots_ref, flags_ref, high_ref, low_ref):
    at = pl.ds(place[0], 1)
    roots = kept_roots(roots_ref[at, :], flags_ref[at, :])
    index = lax.broadcasted_iota(jnp.int32, roots.shape, 1).astype(F32)
    blocks = cols_ref.shape[1] // 2

    def tile(b, near, rows, lanes):
        pole, target = cols_ref[near, b : b + 1], cols_ref[near, blocks + b : blocks + b + 1]
        high_ref[rows, lanes], low_ref[rows, lanes] = split(inverse_gap(pole, target, roots[:, lanes], index[:, lanes]))

    over_tiles(*high_ref.shape, tile)


def table_two_kernel(place, cols_ref, roots_ref, flags_ref, out_ref):
    columns = out_ref.shape[1]
    first = pl.multiple_of(place[2] * columns, LANES)
    roots = kept_roots(roots_ref[:, pl.ds(first, columns)], flags_ref[:, pl.ds(first, columns)])
    index = (lax.broadcasted_iota(jnp.int32, roots.shape, 1) + first).astype(F32)
    blocks = cols_ref.shape[1] // 2

    def tile(b, near, rows, lanes):
        pole, target = cols_ref[near, b : b + 1], cols_ref[near, blocks + b : blocks + b + 1]
        out_ref[rows, lanes] = inverse_gap(pole, target, roots[:, lanes], index[:, lanes])

    over_tiles(*out_ref.shape, tile)


def add_rows(total, x):
    for i in range(0, x.shape[0], 8):
        total = total + x[i : i + 8]
    return total


def norm_one_kernel(place, edge_ref, cols_ref, roots_ref, flags_ref, out_ref, edge_cols):
    pair, side = place[0], place[1]
    at = pl.ds(pair, 1)
    roots = kept_roots(roots_ref[at, :], flags_ref[at, :])
    width = roots.shape[1]
    index = lax.broadcasted_iota(jnp.int32, roots.shape, 1).astype(F32)
    blocks = cols_ref.shape[1] // 2
    edges = edge_ref[...]
    share = edges.shape[1]
    own = jnp.where(side == 0, edges[0:1], edges[1:2])
    other = jnp.where(side == 0, edges[1:2], edges[0:1])
    own_edge = jnp.where(side == 1 - pair, edges[2:3], 0.0)
    other_edge = jnp.where(side == 1 - pair, 0.0, edges[2:3])
    pad = jnp.zeros((4, share), F32)
    rows_all = jnp.concatenate([own, other, own_edge, other_edge, pad], axis=0)
    for b in range(share // LANES):
        edge_cols[b] = rows_all[:, LANES * b : LANES * (b + 1)].T
    for first in range(0, width, WIDTH):
        lanes = slice(first, first + WIDTH)
        carry = (jnp.zeros((8, WIDTH), F32), jnp.zeros((8, WIDTH), F32))
        for part in range(2):
            for b in range(share // LANES):
                block = part * (blocks // 2) + b

                def step(i, carry, part=part, b=b, block=block, lanes=lanes):
                    rows = pl.ds(pl.multiple_of(i * ROWS, ROWS), ROWS)
                    target = cols_ref[rows, blocks + block : blocks + block + 1]
                    gap = pltpu.reciprocal(cols_ref[rows, block : block + 1] - roots[:, lanes], approx=True)
                    z = edge_cols[b, rows, part : part + 1]
                    edge = edge_cols[b, rows, 2 + part : 3 + part]
                    scaled = z * gap
                    weighed = edge * jnp.where(target == index[:, lanes], 1.0, scaled)
                    return add_rows(carry[0], scaled * scaled), add_rows(carry[1], weighed)

                carry = lax.fori_loop(0, LANES // ROWS, step, carry, unroll=LANES // ROWS)
        out_ref[0:1, lanes] = jnp.sum(carry[0], axis=0, keepdims=True)
        out_ref[1:2, lanes] = jnp.sum(carry[1], axis=0, keepdims=True)
    out_ref[2:3, :] = jnp.concatenate([own, jnp.zeros((1, width - share), F32)], axis=1)
    out_ref[3:4, :] = jnp.zeros((1, width), F32)


def weight_kernel(place, here, near, far, last, flags_ref, one_cols, two_cols, out_ref):
    pieces = [here, near, far, last]
    share = here.shape[1] // 8
    squares = sum(p[0:1, :] for p in pieces)
    edge = sum(p[1:2, :] for p in pieces)
    gone = flags_ref[pl.ds(place[0], 1), :] > 0
    scale = jnp.where(gone, 1.0, lax.rsqrt(squares + 1e-06))
    blocks = two_cols.shape[1] // 2
    scale = as_columns(scale)
    z_two = as_columns(edge) * scale
    row_gone = two_cols[:, blocks:] >= 0.0
    out_ref[:, 0:blocks] = scale * jnp.where(row_gone, 1.0, z_two)
    out_ref[:, blocks : 2 * blocks] = jnp.where(row_gone, 0.0, z_two)
    z_one = as_columns(jnp.concatenate([p[2:3, 0:share] for p in pieces], axis=1))
    row_gone = one_cols[:, blocks : blocks + blocks // 2] >= 0.0
    out_ref[:, 2 * blocks : 2 * blocks + blocks // 2] = jnp.where(row_gone, 1.0, z_one)


def mid_kernel(part, weights, high_ref, low_ref, two_ref, mid_high, mid_low, squares_ref, b_high, b_low):
    depth, columns = b_high.shape
    blocks = depth // LANES
    for first in range(0, columns, WIDTH):
        lanes = slice(first, first + WIDTH)
        from_lanes = slice(part * columns + first, part * columns + first + WIDTH)
        squares = jnp.zeros((8, WIDTH), F32)
        for b in range(blocks):

            def step(i, squares, b=b, lanes=lanes, from_lanes=from_lanes):
                rows = pl.ds(pl.multiple_of(i * ROWS, ROWS), ROWS)
                to = pl.ds(pl.multiple_of(b * LANES + i * ROWS, ROWS), ROWS)
                table = two_ref[to, from_lanes]
                b_high[to, lanes], b_low[to, lanes] = split(table * weights[rows, b : b + 1])
                scaled = table * weights[rows, blocks + b : blocks + b + 1]
                return add_rows(squares, scaled * scaled)

            squares = lax.fori_loop(0, LANES // ROWS, step, squares, unroll=LANES // ROWS)
        squares_ref[:, lanes] = jnp.sum(squares, axis=0, keepdims=True)
    for b in range(mid_high.shape[0] // 256):
        rows = slice(256 * b, 256 * (b + 1))
        mid = dot3(high_ref[rows, :], low_ref[rows, :], b_high[...], b_low[...])
        for part in range(2):
            at = 2 * blocks + 2 * b + part
            to = slice(256 * b + LANES * part, 256 * b + LANES * (part + 1))
            mid_high[to, :], mid_low[to, :] = split(mid[LANES * part : LANES * (part + 1)] * weights[:, at : at + 1])


def apply_kernel(count, *refs):
    pieces, (left_high, left_low, right_high, right_low, out_ref) = refs[:count], refs[count:]
    share = pieces[0].shape[1]
    for i, (mid_high, mid_low) in enumerate(((left_high, left_low), (right_high, right_low))):
        width = mid_high.shape[1]
        total = None
        for k, piece in enumerate(pieces):
            rows = slice(share * k, share * (k + 1))
            term = dot3(*split(piece[...]), mid_high[rows, :], mid_low[rows, :])
            total = term if total is None else total + term
        out_ref[:, width * i : width * (i + 1)] = total


def finish_kernel(place, total_ref, mine, other, squares_left, squares_right, squares_far, flags_ref,
                  left_high, left_low, right_high, right_low, out_ref):
    columns = out_ref.shape[1]
    share = mine.shape[1]
    flags = flags_ref[:, pl.ds(pl.multiple_of(place[2] * columns, LANES), columns)]
    squares = jnp.concatenate([squares_left[...], squares_right[...]], axis=1) + squares_far[...]
    scale = jnp.where(flags > 0, 1.0, lax.rsqrt(squares + 1e-06))
    high, low = split(mine[...] + other[...])
    for i, (mid_high, mid_low) in enumerate(((left_high, left_low), (right_high, right_low))):
        width = mid_high.shape[1]
        at = slice(width * i, width * (i + 1))
        rows = slice(share * 3, share * 4)
        term = dot3(high, low, mid_high[rows, :], mid_low[rows, :])
        out_ref[:, at] = (total_ref[:, at] + term) * scale[:, at]


SMEM = pl.BlockSpec(memory_space=pltpu.SMEM)
VMEM = pl.BlockSpec(memory_space=pltpu.VMEM)


def call(kernel, name, outs, inputs, flops=0, scratch=()):
    shapes = [(jax.ShapeDtypeStruct if name == "finish" else pltpu.VMEM)(shape, kind) for shape, kind in outs]
    moved = sum(x.size * x.dtype.itemsize for x in inputs) + sum(math.prod(s) * jnp.dtype(k).itemsize for s, k in outs)
    return pl.pallas_call(
        kernel,
        name=name,
        out_shape=shapes,
        in_specs=[SMEM if x.size == 4 else VMEM for x in inputs],
        out_specs=[VMEM] * len(shapes),
        scratch_shapes=list(scratch),
        cost_estimate=pl.CostEstimate(flops=flops, bytes_accessed=moved, transcendentals=0),
        compiler_params=pltpu.CompilerParams(vmem_limit_bytes=SOME_VMEM),
    )(*inputs)


def body(vectors_in, poles_one, roots_one, order_one, deflate_one, poles_two, roots_two, order_two, deflate_two):
    row_total = lax.axis_size("row")
    assert lax.axis_size("col") == 4
    row_place = lax.axis_index("row")
    col_place = lax.axis_index("col")
    local_rows, share = vectors_in.shape
    leaf = 4 * share
    width_one = 2 * leaf
    width_two = 4 * leaf
    columns = width_two // 4
    per_leaf = row_total // 4
    leaf_number = row_place // per_leaf
    pair = leaf_number // 2
    side = leaf_number % 2
    place = jnp.stack([pair, side, col_place, row_place]).astype(jnp.int32)
    roots_two, order_two, poles_two, deflate_two = (
        a.reshape(1, width_two) for a in (roots_two, order_two, poles_two, deflate_two)
    )

    def along_col(x, moves):
        return lax.ppermute(x, "col", moves)

    far = along_col(vectors_in, [(0, 2), (1, 3), (2, 0), (3, 1)])
    near = along_col(vectors_in, [(0, 1), (1, 0), (2, 3), (3, 2)])

    first_row, last_row = vectors_in[0:1], vectors_in[local_rows - 1 :]
    start = 2 * pair * per_leaf
    edges = jnp.concatenate(
        [
            jnp.where(row_place == start + per_leaf - 1, last_row, 0.0),
            jnp.where(row_place == start + per_leaf, first_row, 0.0),
            jnp.where(row_place == 2 * per_leaf - 1, last_row, jnp.where(row_place == 2 * per_leaf, first_row, 0.0)),
            jnp.zeros((5, share), F32),
        ],
        axis=0,
    )
    step = 1
    while step < 2 * per_leaf:
        edges = edges + lax.ppermute(edges, "row", [(i, i ^ step) for i in range(row_total)])
        step *= 2

    blocks = width_one // LANES
    one_cols, two_cols = call(
        perm_kernel, "orders", [((LANES, 2 * blocks), F32)] * 2,
        [place, order_one, poles_one, deflate_one, order_two, poles_two, deflate_two],
    )
    one_high, one_low = call(
        table_one_kernel, "table_one", [((leaf, width_one), BF16)] * 2,
        [place, one_cols, roots_one, deflate_one], flops=10 * leaf * width_one,
    )
    (table_two,) = call(
        table_two_kernel, "table_two", [((width_one, columns), F32)],
        [place, two_cols, roots_two, deflate_two], flops=10 * width_one * columns,
    )
    (sums,) = call(
        norm_one_kernel, "norm_one", [((4, width_one), F32)],
        [place, edges, one_cols, roots_one, deflate_one], flops=10 * 2 * share * width_one,
        scratch=[pltpu.VMEM((share // LANES, LANES, 8), F32)],
    )
    sums_moved = [along_col(sums, [(i, i ^ k) for i in range(4)]) for k in (1, 2, 3)]
    (weights,) = call(
        weight_kernel, "weights", [((LANES, 2 * blocks + blocks // 2), F32)],
        [place, sums, *sums_moved, deflate_one, one_cols, two_cols],
    )
    weights, far = lax.optimization_barrier((weights, far))
    halves = []
    squares = []
    width = columns // 2
    for i in range(2):
        mid_high, mid_low, part = call(
            functools.partial(mid_kernel, i), "mid", [((leaf, width), BF16)] * 2 + [((1, width), F32)],
            [weights, one_high, one_low, table_two],
            flops=6 * leaf * width_one * width,
            scratch=[pltpu.VMEM((width_one, width), BF16)] * 2,
        )
        halves += [mid_high, mid_low]
        squares.append(part)
    half_row = row_total // 2
    squares_far = lax.ppermute(
        jnp.concatenate(squares, axis=1), "row", [(i, (i + half_row) % row_total) for i in range(row_total)]
    )
    third = along_col(far, [(1, 0), (2, 3)])
    fourth = along_col(vectors_in, [(1, 2), (2, 1)])
    (total,) = call(
        functools.partial(apply_kernel, 3), "apply", [((local_rows, columns), F32)],
        [vectors_in, near, far, *halves], flops=6 * local_rows * 3 * share * columns,
    )
    (merged,) = call(
        finish_kernel, "finish", [((local_rows, columns), F32)],
        [place, total, third, fourth, *squares, squares_far, deflate_two, *halves],
        flops=6 * local_rows * share * columns,
    )
    return merged


def solution(mesh):
    placed = (P("row", "col"), P(), P(), P(), P(), P(), P(), P(), P())
    return jax.shard_map(body, mesh=mesh, in_specs=placed, out_specs=P("row", "col"), check_vma=False)
```

time: 352 us -> 57.3 us (0.16)
  local copies, waits for them, and re-layouts: 175 us -> 5.82 us
  matrix products: 71.8 us -> 0 us
  blocking collectives: 53 us -> 0 us
  other arithmetic: 32.9 us -> 1.02 us
  Pallas kernels: 0 us -> 29.3 us
  starting transfers between devices: 0.04 us -> 14.7 us
  between operations: 13.7 us -> 0.15 us
  waiting for transfers between devices: 0.77 us -> 5.27 us
  loops' own time: 4.26 us -> 0 us
    gather x144 -> x0, local copies, waits for them, and re-layouts: 165 us -> none  [the longest x48 55.1 us: add_squares(): jnp.take(kept_mask, inv_rows)[:, None] * cauchy * cauchy]
    dot_general x24 -> x0, matrix products: 71.8 us -> none  [add_block(): jnp.dot(part_cols, factors, precision=lax.Precision.HIGHEST, preferred_el...]
    pallas_call x0 -> x9, Pallas kernels: none -> 29.3 us  [call(): pl.pallas_call(kernel, name=name, out_shape=shapes, in_specs=[SMEM if x.s...]
    psum x2 -> x0, blocking collectives: 26.9 us -> none  [the longest x1 15.1 us: body(): row_summed = lax.psum(edge_part, 'row')]
    all_gather x2 -> x0, blocking collectives: 26.1 us -> none  [the longest x1 13.3 us: body(): edges_two = lax.all_gather(rows_two, 'col', axis=1, tiled=True)]
    ppermute x0 -> x10, starting transfers between devices: none -> 14.7 us  [the longest x7 11 us: along_col(): return lax.ppermute(x, 'col', moves)]
    sort x2 -> x0, other arithmetic: 10.8 us -> none  [setup_level(): inverse = jnp.argsort(order_vals)]
    select_n x144 -> x1, other arithmetic: 9.64 us -> 0.72 us  [body(): jnp.where(row_place == start + per_leaf - 1, last_row, 0.0)]
  transfers between devices with their start and end apart: 2 -> 10, of which waited for: 0 -> 2; matrix products, arithmetic and copies ran while one was open for 42% -> 0% of each run, Pallas kernels for 0% -> 47%
where the time goes in v1:
time: 57.3 us; the launch traced here: 56.3 us
  Pallas kernels  29.3 us (51%)
  starting transfers between devices  14.7 us (26%)
  local copies, waits for them, and re-layouts  5.82 us (10%)
  waiting for transfers between devices  5.27 us (9%)
  other arithmetic  1.02 us (2%)
    pallas_call x9, Pallas kernels, call(): pl.pallas_call(kernel, name=name, out_shape=shapes, in_specs=[SMEM if x.s...  29.3 us
    ppermute x7, starting transfers between devices, along_col(): return lax.ppermute(x, 'col', moves)  11 us
    unnamed x20, local copies, waits for them, and re-layouts  5.74 us
    ppermute x7, waiting for transfers between devices, along_col(): return lax.ppermute(x, 'col', moves)  5.27 us
    ppermute x2, starting transfers between devices, body(): lax.ppermute(edges, 'row', [(i, i ^ step) for i in range(row_total)])  1.95 us
    ppermute x1, starting transfers between devices, body(): lax.ppermute(jnp.concatenate(squares, axis=1), 'row', [(i, (i + half_row)...  1.83 us
  transfers between devices with their start and end apart: 10, of which 2 were waited for; matrix products, arithmetic and copies ran while one was open for 0% of the time, Pallas kernels for 47%

profile of v1, /device:TPU:0, one launch (start us, length us, event | category | flops | bytes accessed | tf_op | source)
XLA Modules:
  0.0 56.3 jit_solution(8151347785693088972)
XLA Ops:
  0.1 0.7 %broadcast_select_fusion.3 = (f32[1,256]{1,0:T(1,128)S(1)}, f32[1,256]{1,0:T(1,128)S(1)}, f32[1,256]{1,0:T(1,128)S(1)}) fusion(pred[]{:T(512)S(6)} %eq.14, f32[512,256]{1,0:T(8,128)} %refs_0_.1, pred[]{:T(512)S(6)} %eq.17, pred[]{:T(512)S(6)} %eq.16, pred[]{:T(512)S(6)} %eq.15), kind=kLoop, calls=%fused_computation.5 | loop fusion | flops 1024 | bytes 5124 | tf_op jit(solution)/shard_map/jit(_where)/select_n | solution.py:295
  1.3 3.7 %collective-permute-start.6 = (f32[512,256]{1,0:T(8,128)}, f32[512,256]{1,0:T(8,128)S(1)}, u32[]{:S(2)}, u32[]{:S(2)}) collective-permute-start(f32[512,256]{1,0:T(8,128)} %refs_0_.1), channel_id=1, source_target_pairs={{0,2},{1,3},{2,0},{3,1},{4,6},{5,7},{6,4},{7,5},{8,10},{9,11},{10,... | collective-permute-start | bytes 1572872 | tf_op jit(solution)/shard_map/ppermute | solution.py:286
  5.1 1.5 %collective-permute-start.2 = (f32[8,256]{1,0:T(8,128)S(1)}, f32[8,256]{1,0:T(8,128)S(1)}, u32[]{:S(2)}, u32[]{:S(2)}) collective-permute-start(f32[8,256]{1,0:T(8,128)S(1)} %fusion), channel_id=1, source_target_pairs={{0,8},{4,12},{8,0},{12,4},{16,24},{20,28},{24,16},{28,20},{1,9},{5... | collective-permute-start | bytes 24584 | tf_op jit(solution)/shard_map/ppermute | solution.py:304
  6.6 0.7 %copy-done = s32[2,2048]{1,0:T(2,128)S(1)} copy-done((s32[2,2048]{1,0:T(2,128)S(1)}, s32[2,2048]{1,0:T(2,128)}, u32[]{:S(2)}) %copy-start) | copy-done | bytes 16408
  7.4 0.7 %copy-done.1 = s32[4096]{0:T(1024)S(1)} copy-done((s32[4096]{0:T(1024)S(1)}, s32[4096]{0:T(1024)}, u32[]{:S(2)}) %copy-start.1) | copy-done | bytes 16408
  8.1 0.7 %copy-done.5 = s32[2,2048]{1,0:T(2,128)S(1)} copy-done((s32[2,2048]{1,0:T(2,128)S(1)}, s32[2,2048]{1,0:T(2,128)}, u32[]{:S(2)}) %copy-start.5) | copy-done | bytes 16408
  8.8 0.7 %copy-done.6 = f32[2,2048]{1,0:T(2,128)S(1)} copy-done((f32[2,2048]{1,0:T(2,128)S(1)}, f32[2,2048]{1,0:T(2,128)}, u32[]{:S(2)}) %copy-start.6) | copy-done | bytes 16408
  11.0 1.3 %orders.1 = (f32[128,32]{1,0:T(8,128)S(1)}, f32[128,32]{1,0:T(8,128)S(1)}) custom-call(s32[4]{0:T(128)S(1)} %pad_add_fusion.place, s32[2,2048]{1,0:T(2,128)S(1)} %copy-done.5, f32[2,2048]{1,0:T(2,128)S(1)} %copy-done.6, s32[2,2048]{1,0:T(2,128)S(1)} %copy-done, s32[1,4096]{1,0:T(1,128)S(1)} %bitcast.12, f32[1,4096]{1,0:T(1,128)S(1)} %bitcast.13, ...), custom_call_target="tpu_custom_call" | custom-call | bytes 131088 | tf_op jit(solution)/shard_map/orders/pallas_call | solution.py:254
  12.3 0.7 %copy-done.3 = f32[2,2048]{1,0:T(2,128)S(1)} copy-done((f32[2,2048]{1,0:T(2,128)S(1)}, f32[2,2048]{1,0:T(2,128)}, u32[]{:S(2)}) %copy-start.3) | copy-done | bytes 16408
  13.0 2.4 %norm_one.1.here = f32[4,2048]{1,0:T(4,128)S(1)} custom-call(s32[4]{0:T(128)S(1)} %pad_add_fusion.place, f32[8,256]{1,0:T(8,128)S(1)} %fusion.1.edge_ref, f32[128,32]{1,0:T(8,128)S(1)} %get-tuple-element.17.cols_ref.one_cols, f32[2,2048]{1,0:T(2,128)S(1)} %copy-done.3, s32[2,2048]{1,0:T(2,128)S(1)} %copy-done), custom_call_target="tpu_custom_call" | custom-call | flops 10485760 | bytes 90128 | tf_op jit(solution)/shard_map/norm_one/pallas_call | solution.py:254
  15.4 1.6 %collective-permute-start.3 = (f32[4,2048]{1,0:T(4,128)S(1)}, f32[4,2048]{1,0:T(4,128)S(1)}, u32[]{:S(2)}, u32[]{:S(2)}) collective-permute-start(f32[4,2048]{1,0:T(4,128)S(1)} %norm_one.1.here), channel_id=1, source_target_pairs={{0,1},{1,0},{2,3},{3,2},{4,5},{5,4},{6,7},{7,6},{8,9},{9,8},{10,11... | collective-permute-start | bytes 98312 | tf_op jit(solution)/shard_map/ppermute | solution.py:286
  17.0 1.1 %collective-permute-start.4 = (f32[4,2048]{1,0:T(4,128)S(1)}, f32[4,2048]{1,0:T(4,128)S(1)}, u32[]{:S(2)}, u32[]{:S(2)}) collective-permute-start(f32[4,2048]{1,0:T(4,128)S(1)} %norm_one.1.here), channel_id=1, source_target_pairs={{0,2},{1,3},{2,0},{3,1},{4,6},{5,7},{6,4},{7,5},{8,10},{9,11},{10,... | collective-permute-start | bytes 98312 | tf_op jit(solution)/shard_map/ppermute | solution.py:286
  18.1 1.7 %collective-permute-start.5 = (f32[4,2048]{1,0:T(4,128)S(1)}, f32[4,2048]{1,0:T(4,128)S(1)}, u32[]{:S(2)}, u32[]{:S(2)}) collective-permute-start(f32[4,2048]{1,0:T(4,128)S(1)} %norm_one.1.here), channel_id=1, source_target_pairs={{0,3},{1,2},{2,1},{3,0},{4,7},{5,6},{6,5},{7,4},{8,11},{9,10},{10,... | collective-permute-start | bytes 98312 | tf_op jit(solution)/shard_map/ppermute | solution.py:286
  20.5 2.8 %table_one.1 = (bf16[1024,2048]{1,0:T(8,128)(2,1)S(1)}, bf16[1024,2048]{1,0:T(8,128)(2,1)S(1)}) custom-call(s32[4]{0:T(128)S(1)} %pad_add_fusion.place, f32[128,32]{1,0:T(8,128)S(1)} %get-tuple-element.17.cols_ref.one_cols, f32[2,2048]{1,0:T(2,128)S(1)} %copy-done.3, s32[2,2048]{1,0:T(2,128)S(1)} %copy-done), custom_call_target="tpu_custom_call" | custom-call | flops 20971520 | bytes 8437776 | tf_op jit(solution)/shard_map/table_one/pallas_call | solution.py:254
  24.0 2.1 %table_two.1.two_ref = f32[2048,1024]{1,0:T(8,128)S(1)} custom-call(s32[4]{0:T(128)S(1)} %pad_add_fusion.place, f32[128,32]{1,0:T(8,128)S(1)} %get-tuple-element.18.two_cols.cols_ref, f32[1,4096]{1,0:T(1,128)S(1)} %bitcast.11, s32[1,4096]{1,0:T(1,128)S(1)} %bitcast.9), custom_call_target="tpu_custom_call" | custom-call | flops 20971520 | bytes 8437776 | tf_op jit(solution)/shard_map/table_two/pallas_call | solution.py:254
  26.9 4.5 %collective-permute-done.4.far = f32[4,2048]{1,0:T(4,128)S(1)} collective-permute-done((f32[4,2048]{1,0:T(4,128)S(1)}, f32[4,2048]{1,0:T(4,128)S(1)}, u32[]{:S(2)}, u32[]{:S(2)}) %collective-permute-start.4) | collective-permute-done | bytes 32800 | tf_op jit(solution)/shard_map/ppermute | solution.py:286
  31.3 0.8 %weights.1 = f32[128,40]{1,0:T(8,128)S(1)} custom-call(s32[4]{0:T(128)S(1)} %pad_add_fusion.place, f32[4,2048]{1,0:T(4,128)S(1)} %norm_one.1.here, f32[4,2048]{1,0:T(4,128)S(1)} %collective-permute-done.3.near, f32[4,2048]{1,0:T(4,128)S(1)} %collective-permute-done.4.far, f32[4,2048]{1,0:T(4,128)S(1)} %collective-permute-done.5.last, s32[2,2048]{1,0:T(2,128)S(1)} %copy-done, ...), custom_call_target="tpu_custom_call" | custom-call | bytes 200720 | tf_op jit(solution)/shard_map/weights/pallas_call | solution.py:254
  32.2 1.5 %collective-permute-start.7 = (f32[512,256]{1,0:T(8,128)S(1)}, f32[512,256]{1,0:T(8,128)S(1)}, u32[]{:S(2)}, u32[]{:S(2)}) collective-permute-start(f32[512,256]{1,0:T(8,128)S(1)} %collective-permute-done.6.refs_2_), channel_id=1, source_target_pairs={{1,0},{2,3},{5,4},{6,7},{9,8},{10,11},{13,12},{14,15},{17,16},{18,... | collective-permute-start | bytes 1572872 | tf_op jit(solution)/shard_map/ppermute | solution.py:286
  33.7 7.2 %mid.3 = (bf16[1024,512]{1,0:T(8,128)(2,1)S(1)}, bf16[1024,512]{1,0:T(8,128)(2,1)S(1)}, f32[1,512]{1,0:T(1,128)S(1)}) custom-call(f32[128,40]{1,0:T(8,128)S(1)} %weights.1, bf16[1024,2048]{1,0:T(8,128)(2,1)S(1)} %get-tuple-element.21.high_ref, bf16[1024,2048]{1,0:T(8,128)(2,1)S(1)} %get-tuple-element.22.low_ref, f32[2048,1024]{1,0:T(8,128)S(1)} %table_two.1.two_ref), custom_call_target="tpu_custom_call" | custom-call | flops 6442450944 | bytes 18896896 | tf_op jit(solution)/shard_map/mid/pallas_call | solution.py:254
  40.9 7.2 %mid.2 = (bf16[1024,512]{1,0:T(8,128)(2,1)S(1)}, bf16[1024,512]{1,0:T(8,128)(2,1)S(1)}, f32[1,512]{1,0:T(1,128)S(1)}) custom-call(f32[128,40]{1,0:T(8,128)S(1)} %weights.1, bf16[1024,2048]{1,0:T(8,128)(2,1)S(1)} %get-tuple-element.21.high_ref, bf16[1024,2048]{1,0:T(8,128)(2,1)S(1)} %get-tuple-element.22.low_ref, f32[2048,1024]{1,0:T(8,128)S(1)} %table_two.1.two_ref), custom_call_target="tpu_custom_call" | custom-call | flops 6442450944 | bytes 18896896 | tf_op jit(solution)/shard_map/mid/pallas_call | solution.py:254
  48.1 1.8 %collective-permute-start.9 = (f32[1,1024]{1,0:T(1,128)S(1)}, f32[1,1024]{1,0:T(1,128)S(1)}, u32[]{:S(2)}, u32[]{:S(2)}) collective-permute-start(f32[1,1024]{1,0:T(1,128)S(1)} %pad_maximum_fusion), channel_id=1, source_target_pairs={{0,16},{4,20},{8,24},{12,28},{16,0},{20,4},{24,8},{28,12},{1,17},{... | collective-permute-start | bytes 12296 | tf_op jit(solution)/shard_map/ppermute | solution.py:344
  50.0 2.6 %apply.1.total_ref = f32[512,1024]{1,0:T(8,128)S(1)} custom-call(f32[512,256]{1,0:T(8,128)S(1)} %copy-done.9, f32[512,256]{1,0:T(8,128)S(1)} %collective-permute-done.refs_1_, f32[512,256]{1,0:T(8,128)S(1)} %collective-permute-done.6.refs_2_, bf16[1024,512]{1,0:T(8,128)(2,1)S(1)} %get-tuple-element.23.refs_3_.left_high, ...), custom_call_target="tpu_custom_call" | custom-call | flops 2415919104 | bytes 7864320 | tf_op jit(solution)/shard_map/apply/pallas_call | solution.py:254
  52.6 0.8 %collective-permute-done.7.mine = f32[512,256]{1,0:T(8,128)S(1)} collective-permute-done((f32[512,256]{1,0:T(8,128)S(1)}, f32[512,256]{1,0:T(8,128)S(1)}, u32[]{:S(2)}, u32[]{:S(2)}) %collective-permute-start.7) | collective-permute-done | bytes 524320 | tf_op jit(solution)/shard_map/ppermute | solution.py:286
  53.4 2.9 %finish.1 = f32[512,1024]{1,0:T(8,128)} custom-call(s32[4]{0:T(128)S(1)} %pad_add_fusion.place, f32[512,1024]{1,0:T(8,128)S(1)} %apply.1.total_ref, f32[512,256]{1,0:T(8,128)S(1)} %collective-permute-done.7.mine, f32[512,256]{1,0:T(8,128)S(1)} %collective-permute-done.8.other, f32[1,512]{1,0:T(1,128)S(1)} %get-tuple-element.27.squares_left, ...), custom_call_target="tpu_custom_call" | custom-call | flops 805306368 | bytes 9461776 | tf_op jit(solution)/shard_map/finish/pallas_call | solution.py:254
  (33 shorter events, 4.4 us)
Async XLA Ops:
  0.9 4.1 %collective-permute-start.1 = (f32[8,256]{1,0:T(8,128)S(1)}, f32[8,256]{1,0:T(8,128)S(1)}, u32[]{:S(2)}, u32[]{:S(2)}) collective-permute-start(f32[8,256]{1,0:T(8,128)S(1)} %maximum_maximum_fusion), channel_id=1, source_target_pairs={{0,4},{4,0},{8,12},{12,8},{16,20},{20,16},{24,28},{28,24},{1,5},{5... | collective-permute-start | bytes 24584 | tf_op jit(solution)/shard_map/ppermute | solution.py:304
  1.3 30.9 %collective-permute-start.6 = (f32[512,256]{1,0:T(8,128)}, f32[512,256]{1,0:T(8,128)S(1)}, u32[]{:S(2)}, u32[]{:S(2)}) collective-permute-start(f32[512,256]{1,0:T(8,128)} %refs_0_.1), channel_id=1, source_target_pairs={{0,2},{1,3},{2,0},{3,1},{4,6},{5,7},{6,4},{7,5},{8,10},{9,11},{10,... | collective-permute-start | bytes 1572872 | tf_op jit(solution)/shard_map/ppermute | solution.py:286
  5.1 7.1 %collective-permute-start.2 = (f32[8,256]{1,0:T(8,128)S(1)}, f32[8,256]{1,0:T(8,128)S(1)}, u32[]{:S(2)}, u32[]{:S(2)}) collective-permute-start(f32[8,256]{1,0:T(8,128)S(1)} %fusion), channel_id=1, source_target_pairs={{0,8},{4,12},{8,0},{12,4},{16,24},{20,28},{24,16},{28,20},{1,9},{5... | collective-permute-start | bytes 24584 | tf_op jit(solution)/shard_map/ppermute | solution.py:304
  6.6 0.7 %copy-start = (s32[2,2048]{1,0:T(2,128)S(1)}, s32[2,2048]{1,0:T(2,128)}, u32[]{:S(2)}) copy-start(s32[2,2048]{1,0:T(2,128)} %flags_ref.5) | copy-start | bytes 49156
  7.4 0.7 %copy-start.1 = (s32[4096]{0:T(1024)S(1)}, s32[4096]{0:T(1024)}, u32[]{:S(2)}) copy-start(s32[4096]{0:T(1024)} %param.17) | copy-start | bytes 49156
  8.1 0.7 %copy-start.5 = (s32[2,2048]{1,0:T(2,128)S(1)}, s32[2,2048]{1,0:T(2,128)}, u32[]{:S(2)}) copy-start(s32[2,2048]{1,0:T(2,128)} %order_one.1) | copy-start | bytes 49156
  8.8 0.7 %copy-start.6 = (f32[2,2048]{1,0:T(2,128)S(1)}, f32[2,2048]{1,0:T(2,128)}, u32[]{:S(2)}) copy-start(f32[2,2048]{1,0:T(2,128)} %poles_one.1) | copy-start | bytes 49156
  9.5 0.7 %copy-start.7 = (s32[4096]{0:T(1024)S(1)}, s32[4096]{0:T(1024)}, u32[]{:S(2)}) copy-start(s32[4096]{0:T(1024)} %param.16) | copy-start | bytes 49156
  10.2 0.7 %copy-start.8 = (f32[4096]{0:T(1024)S(1)}, f32[4096]{0:T(1024)}, u32[]{:S(2)}) copy-start(f32[4096]{0:T(1024)} %param.14) | copy-start | bytes 49156
  12.3 0.7 %copy-start.3 = (f32[2,2048]{1,0:T(2,128)S(1)}, f32[2,2048]{1,0:T(2,128)}, u32[]{:S(2)}) copy-start(f32[2,2048]{1,0:T(2,128)} %roots_ref.3) | copy-start | bytes 49156
  15.4 10.8 %collective-permute-start.3 = (f32[4,2048]{1,0:T(4,128)S(1)}, f32[4,2048]{1,0:T(4,128)S(1)}, u32[]{:S(2)}, u32[]{:S(2)}) collective-permute-start(f32[4,2048]{1,0:T(4,128)S(1)} %norm_one.1.here), channel_id=1, source_target_pairs={{0,1},{1,0},{2,3},{3,2},{4,5},{5,4},{6,7},{7,6},{8,9},{9,8},{10,11... | collective-permute-start | bytes 98312 | tf_op jit(solution)/shard_map/ppermute | solution.py:286
  17.0 14.3 %collective-permute-start.4 = (f32[4,2048]{1,0:T(4,128)S(1)}, f32[4,2048]{1,0:T(4,128)S(1)}, u32[]{:S(2)}, u32[]{:S(2)}) collective-permute-start(f32[4,2048]{1,0:T(4,128)S(1)} %norm_one.1.here), channel_id=1, source_target_pairs={{0,2},{1,3},{2,0},{3,1},{4,6},{5,7},{6,4},{7,5},{8,10},{9,11},{10,... | collective-permute-start | bytes 98312 | tf_op jit(solution)/shard_map/ppermute | solution.py:286
  18.1 13.2 %collective-permute-start.5 = (f32[4,2048]{1,0:T(4,128)S(1)}, f32[4,2048]{1,0:T(4,128)S(1)}, u32[]{:S(2)}, u32[]{:S(2)}) collective-permute-start(f32[4,2048]{1,0:T(4,128)S(1)} %norm_one.1.here), channel_id=1, source_target_pairs={{0,3},{1,2},{2,1},{3,0},{4,7},{5,6},{6,5},{7,4},{8,11},{9,10},{10,... | collective-permute-start | bytes 98312 | tf_op jit(solution)/shard_map/ppermute | solution.py:286
  19.8 30.1 %collective-permute-start = (f32[512,256]{1,0:T(8,128)}, f32[512,256]{1,0:T(8,128)S(1)}, u32[]{:S(2)}, u32[]{:S(2)}) collective-permute-start(f32[512,256]{1,0:T(8,128)} %refs_0_.1), channel_id=1, source_target_pairs={{0,1},{1,0},{2,3},{3,2},{4,5},{5,4},{6,7},{7,6},{8,9},{9,8},{10,11... | collective-permute-start | bytes 1572872 | tf_op jit(solution)/shard_map/ppermute | solution.py:286
  23.3 0.7 %copy-start.4 = (f32[4096]{0:T(1024)S(1)}, f32[4096]{0:T(1024)}, u32[]{:S(2)}) copy-start(f32[4096]{0:T(1024)} %param.15) | copy-start | bytes 49156
  24.0 2.1 %copy-start.9 = (f32[512,256]{1,0:T(8,128)S(1)}, f32[512,256]{1,0:T(8,128)}, u32[]{:S(2)}) copy-start(f32[512,256]{1,0:T(8,128)} %refs_0_.1) | copy-start | bytes 1572868
  26.2 26.4 %collective-permute-start.8 = (f32[512,256]{1,0:T(8,128)S(1)}, f32[512,256]{1,0:T(8,128)S(1)}, u32[]{:S(2)}, u32[]{:S(2)}) collective-permute-start(f32[512,256]{1,0:T(8,128)S(1)} %copy-done.9), channel_id=1, source_target_pairs={{1,2},{2,1},{5,6},{6,5},{9,10},{10,9},{13,14},{14,13},{17,18},{18,... | collective-permute-start | bytes 1572872 | tf_op jit(solution)/shard_map/ppermute | solution.py:286
  32.2 21.2 %collective-permute-start.7 = (f32[512,256]{1,0:T(8,128)S(1)}, f32[512,256]{1,0:T(8,128)S(1)}, u32[]{:S(2)}, u32[]{:S(2)}) collective-permute-start(f32[512,256]{1,0:T(8,128)S(1)} %collective-permute-done.6.refs_2_), channel_id=1, source_target_pairs={{1,0},{2,3},{5,4},{6,7},{9,8},{10,11},{13,12},{14,15},{17,16},{18,... | collective-permute-start | bytes 1572872 | tf_op jit(solution)/shard_map/ppermute | solution.py:286
  48.1 4.5 %collective-permute-start.9 = (f32[1,1024]{1,0:T(1,128)S(1)}, f32[1,1024]{1,0:T(1,128)S(1)}, u32[]{:S(2)}, u32[]{:S(2)}) collective-permute-start(f32[1,1024]{1,0:T(1,128)S(1)} %pad_maximum_fusion), channel_id=1, source_target_pairs={{0,16},{4,20},{8,24},{12,28},{16,0},{20,4},{24,8},{28,12},{1,17},{... | collective-permute-start | bytes 12296 | tf_op jit(solution)/shard_map/ppermute | solution.py:344
  50.0 3.4 %copy-start.2 = (s32[4096]{0:T(1024)S(1)}, s32[4096]{0:T(1024)}, u32[]{:S(2)}) copy-start(s32[4096]{0:T(1024)} %param.17) | copy-start | bytes 49156

commit v2 on v1

v2 whole, which is shorter than its diff:
```python
import functools
import math

import jax
import jax.numpy as jnp
from jax import lax
from jax.experimental import pallas as pl
from jax.experimental.pallas import tpu as pltpu
from jax.sharding import PartitionSpec as P

F32 = jnp.float32
BF16 = jnp.bfloat16
LANES = 128
SOME_VMEM = 14 * 1024 * 1024
ROWS, WIDTH = 32, 512
PIECES = (1, 2)
WEIGHTS = {"orders": 100, "table_one": 100, "table_two": 100, "norm_one": 100, "apply": 0.001, "finish": 0.001}


def split(x):
    high = x.astype(BF16)
    return high, (x - high.astype(F32)).astype(BF16)


def dot3(a_high, a_low, b_high, b_low):
    dot = functools.partial(jnp.dot, preferred_element_type=F32)
    return dot(a_high, b_high) + dot(a_low, b_high) + dot(a_high, b_low)


def as_columns(row):
    count = row.shape[1] // LANES
    stacked = jnp.concatenate([row[:, LANES * b : LANES * (b + 1)] for b in range(count)], axis=0)
    return stacked.T


def permuted(order, low_bits, wanted, values):
    at_high = order >> 7 == wanted
    at_low = ((order & 127) == low_bits).astype(BF16)
    rows = jnp.concatenate([jnp.where(at_high, v, 0.0).astype(BF16) for v in values], axis=0)
    out = lax.dot_general(rows, at_low, (((1,), (1,)), ((), ())), preferred_element_type=F32)
    count = wanted.shape[0]
    return [out[count * i : count * (i + 1)] for i in range(len(values))]


def place_tables(order, poles, flags, wanted):
    span = order.shape[1]
    low_bits = lax.broadcasted_iota(jnp.int32, (LANES, span), 0)
    index = lax.broadcasted_iota(jnp.int32, (1, span), 1)
    first = poles.astype(BF16).astype(F32)
    second = (poles - first).astype(BF16).astype(F32)
    third = poles - first - second
    values = [first, second, third, (index >> 6).astype(F32), (index & 63).astype(F32), flags.astype(F32)]
    one, two, three, upper, lower, flag = permuted(order, low_bits, wanted, values)
    gone = flag > 0.5
    pole = jnp.where(gone, jnp.inf, one + two + three)
    target = jnp.where(gone, upper * 64.0 + lower, -1.0)
    return pole, target


def perm_kernel(place, *refs):
    given, outs, (held, arrived) = refs[:8], refs[8:14], (refs[14:22], refs[22])
    one_out, two_out, roots_one_out, flags_one_out, roots_two_out, flags_two_out = outs
    copies = [pltpu.make_async_copy(x, y, arrived.at[i]) for i, (x, y) in enumerate(zip(given, held))]
    for copy in copies:
        copy.start()
    for copy in copies:
        copy.wait()
    poles_one, roots_one, order_one, flags_one, poles_two, roots_two, order_two, flags_two = held
    pair, side, piece, core = place[0], place[1], place[2], place[3]
    blocks = order_one.shape[1] // LANES
    spot = lax.broadcasted_iota(jnp.int32, (blocks, 1), 0)
    half = blocks // 2
    per = half // 4
    late = spot - half // 2
    wanted_one = jnp.where(late < 0, side, 1 - side) * half
    wanted_one += (((spot % (half // 2)) // per) ^ piece ^ (2 * core)) * per + spot % per
    wanted_one = jnp.where(spot < half, wanted_one, -1)
    at = pl.ds(pair, 1)
    flags = flags_one[at, :]
    flags_one_out[...] = flags
    roots_one_out[...] = jnp.where(flags > 0, -jnp.inf, roots_one[at, :])
    pole, target = place_tables(order_one[at, :], poles_one[at, :], flags, wanted_one)
    one_out[...] = jnp.concatenate([pole, target], axis=0).T
    columns = roots_two_out.shape[1]
    lanes = pl.ds(pl.multiple_of(piece * columns, LANES), columns)
    flags = flags_two[:, lanes]
    flags_two_out[...] = flags
    roots_two_out[...] = jnp.where(flags > 0, -jnp.inf, roots_two[:, lanes])
    pole, target = place_tables(order_two[...], poles_two[...], flags_two[...], spot + pair * blocks)
    two_out[...] = jnp.concatenate([pole, target], axis=0).T


def inverse_gap(pole, target, roots, index):
    gap = pltpu.reciprocal(pole - roots, approx=True)
    return jnp.where(target == index, 1.0, gap)


def over_tiles(height, width, tile):
    for first in range(0, width, WIDTH):
        lanes = slice(first, first + WIDTH)
        for b in range(height // LANES):

            def step(i, _, b=b, lanes=lanes):
                near = pl.multiple_of(i * ROWS, ROWS)
                tile(b, pl.ds(near, ROWS), pl.ds(pl.multiple_of(b * LANES + near, ROWS), ROWS), lanes)
                return 0

            lax.fori_loop(0, LANES // ROWS, step, 0, unroll=LANES // ROWS)


def table_one_kernel(cols_ref, roots_ref, high_ref, low_ref):
    roots = roots_ref[...]
    index = lax.broadcasted_iota(jnp.int32, roots.shape, 1).astype(F32)
    blocks = cols_ref.shape[1] // 2

    def tile(b, near, rows, lanes):
        pole, target = cols_ref[near, b : b + 1], cols_ref[near, blocks + b : blocks + b + 1]
        high_ref[rows, lanes], low_ref[rows, lanes] = split(inverse_gap(pole, target, roots[:, lanes], index[:, lanes]))

    over_tiles(*high_ref.shape, tile)


def table_two_kernel(place, cols_ref, roots_ref, out_ref):
    roots = roots_ref[...]
    index = (lax.broadcasted_iota(jnp.int32, roots.shape, 1) + place[2] * out_ref.shape[1]).astype(F32)
    blocks = cols_ref.shape[1] // 2

    def tile(b, near, rows, lanes):
        pole, target = cols_ref[near, b : b + 1], cols_ref[near, blocks + b : blocks + b + 1]
        out_ref[rows, lanes] = inverse_gap(pole, target, roots[:, lanes], index[:, lanes])

    over_tiles(*out_ref.shape, tile)


def add_rows(total, x):
    for i in range(0, x.shape[0], 8):
        total = total + x[i : i + 8]
    return total


def norm_one_kernel(place, edge_ref, cols_ref, roots_ref, out_ref, edge_cols):
    pair, side, core = place[0], place[1], place[3]
    roots = roots_ref[...]
    width = roots.shape[1]
    index = lax.broadcasted_iota(jnp.int32, roots.shape, 1).astype(F32)
    blocks = cols_ref.shape[1] // 2
    share = edge_ref.shape[1] // 2
    edges = edge_ref[:, pl.ds(pl.multiple_of(core * share, LANES), share)]
    own = jnp.where(side == 0, edges[0:1], edges[1:2])
    other = jnp.where(side == 0, edges[1:2], edges[0:1])
    own_edge = jnp.where(side == 1 - pair, edges[2:3], 0.0)
    other_edge = jnp.where(side == 1 - pair, 0.0, edges[2:3])
    pad = jnp.zeros((4, share), F32)
    rows_all = jnp.concatenate([own, other, own_edge, other_edge, pad], axis=0)
    for b in range(share // LANES):
        edge_cols[b] = rows_all[:, LANES * b : LANES * (b + 1)].T
    for first in range(0, width, WIDTH):
        lanes = slice(first, first + WIDTH)
        carry = (jnp.zeros((8, WIDTH), F32), jnp.zeros((8, WIDTH), F32))
        for part in range(2):
            for b in range(share // LANES):
                block = part * (share // LANES) + b

                def step(i, carry, part=part, b=b, block=block, lanes=lanes):
                    rows = pl.ds(pl.multiple_of(i * ROWS, ROWS), ROWS)
                    target = cols_ref[rows, blocks + block : blocks + block + 1]
                    gap = pltpu.reciprocal(cols_ref[rows, block : block + 1] - roots[:, lanes], approx=True)
                    z = edge_cols[b, rows, part : part + 1]
                    edge = edge_cols[b, rows, 2 + part : 3 + part]
                    scaled = z * gap
                    weighed = edge * jnp.where(target == index[:, lanes], 1.0, scaled)
                    return add_rows(carry[0], scaled * scaled), add_rows(carry[1], weighed)

                carry = lax.fori_loop(0, LANES // ROWS, step, carry, unroll=LANES // ROWS)
        out_ref[0:1, lanes] = jnp.sum(carry[0], axis=0, keepdims=True)
        out_ref[1:2, lanes] = jnp.sum(carry[1], axis=0, keepdims=True)


def weight_kernel(place, here, there, edge_ref, flags_ref, one_cols, two_cols, out_ref):
    squares = here[0:1, :] + there[0:1, :]
    edge = here[1:2, :] + there[1:2, :]
    gone = flags_ref[...] > 0
    scale = as_columns(jnp.where(gone, 1.0, lax.rsqrt(squares + 1e-06)))
    blocks = two_cols.shape[1] // 2
    z_two = as_columns(edge) * scale
    row_gone = two_cols[:, blocks:] >= 0.0
    out_ref[:, 0:blocks] = scale * jnp.where(row_gone, 1.0, z_two)
    out_ref[:, blocks : 2 * blocks] = jnp.where(row_gone, 0.0, z_two)
    share = edge_ref.shape[1] // 2
    edges = edge_ref[:, pl.ds(pl.multiple_of(place[3] * share, LANES), share)]
    z_one = as_columns(jnp.where(place[1] == 0, edges[0:1], edges[1:2]))
    count = z_one.shape[1]
    row_gone = one_cols[:, blocks : blocks + count] >= 0.0
    out_ref[:, 2 * blocks : 2 * blocks + count] = jnp.where(row_gone, 1.0, z_one)


def scale_kernel(weights, two_ref, b_high, b_low, squares_ref):
    depth, columns = b_high.shape
    blocks = depth // LANES
    for first in range(0, columns, WIDTH):
        lanes = slice(first, first + WIDTH)
        squares = jnp.zeros((8, WIDTH), F32)
        for b in range(blocks):

            def step(i, squares, b=b, lanes=lanes):
                rows = pl.ds(pl.multiple_of(i * ROWS, ROWS), ROWS)
                to = pl.ds(pl.multiple_of(b * LANES + i * ROWS, ROWS), ROWS)
                table = two_ref[to, lanes]
                b_high[to, lanes], b_low[to, lanes] = split(table * weights[rows, b : b + 1])
                scaled = table * weights[rows, blocks + b : blocks + b + 1]
                return add_rows(squares, scaled * scaled)

            squares = lax.fori_loop(0, LANES // ROWS, step, squares, unroll=LANES // ROWS)
        squares_ref[:, lanes] = jnp.sum(squares, axis=0, keepdims=True)


def mid_kernel(part, weights, high_ref, low_ref, b_high, b_low, *outs):
    piece, columns = outs[0].shape
    height = piece * len(outs)
    blocks = b_high.shape[0] // LANES
    rows = slice(height * part, height * (part + 1))
    for first in range(0, columns, WIDTH):
        lanes = slice(first, first + WIDTH)
        mid = dot3(high_ref[rows, :], low_ref[rows, :], b_high[:, lanes], b_low[:, lanes])
        for i, out_ref in enumerate(outs):
            for begin in range(0, piece, LANES):
                count = min(LANES, piece)
                b, inner = divmod(piece * i + begin, LANES)
                at = 2 * blocks + part * (height // LANES) + b
                scale = weights[inner : inner + count, at : at + 1]
                out_ref[begin : begin + count, lanes] = mid[piece * i + begin : piece * i + begin + count] * scale


def apply_kernel(place, own_mid, other_mid, mine, far, out_ref):
    first = place[3] == 0
    own = split(jnp.where(first, mine[...], far[...]))
    other = split(jnp.where(first, far[...], mine[...]))
    for at in range(0, out_ref.shape[1], WIDTH):
        lanes = slice(at, at + WIDTH)
        out_ref[:, lanes] = dot3(*own, *split(own_mid[:, lanes])) + dot3(*other, *split(other_mid[:, lanes]))


def finish_kernel(place, near_ref, last_end, last_middle, total_ref, squares, squares_far, flags_ref, *refs):
    count = len(refs) // 2 - 1
    own_late, other_late, (out_ref, done, left) = refs[:count], refs[count : 2 * count], refs[2 * count :]
    scale = jnp.where(flags_ref[...] > 0, 1.0, lax.rsqrt(squares[...] + squares_far[...] + 1e-06))
    first = place[3] == 0
    near, last = near_ref[...], last_end[...] + last_middle[...]
    own = split(jnp.where(first, near, last))
    other = split(jnp.where(first, last, near))
    copies = []
    for i, at in enumerate(range(0, out_ref.shape[1], WIDTH)):
        lanes = slice(at, at + WIDTH)
        own_mid = jnp.concatenate([x[:, lanes] for x in own_late], axis=0)
        other_mid = jnp.concatenate([x[:, lanes] for x in other_late], axis=0)
        term = dot3(*own, *split(own_mid)) + dot3(*other, *split(other_mid))
        done[:, lanes] = (total_ref[:, lanes] + term) * scale[:, lanes]
        copies.append(pltpu.make_async_copy(done.at[:, lanes], out_ref.at[:, lanes], left.at[i]))
        copies[-1].start()
    for copy in copies:
        copy.wait()


SMEM = pl.BlockSpec(memory_space=pltpu.SMEM)
VMEM = pl.BlockSpec(memory_space=pltpu.VMEM)
HBM = pl.BlockSpec(memory_space=pltpu.HBM)


def call(kernel, name, outs, inputs, flops=0, scratch=()):
    shapes = [(jax.ShapeDtypeStruct if name == "finish" else pltpu.VMEM)(shape, kind) for shape, kind in outs]
    weight = WEIGHTS.get(name, 1)
    moved = sum(x.size * x.dtype.itemsize for x in inputs) + sum(math.prod(s) * jnp.dtype(k).itemsize for s, k in outs)
    return pl.pallas_call(
        kernel,
        name=name,
        out_shape=shapes,
        in_specs=[SMEM if x.size == 4 else HBM if name == "orders" else VMEM for x in inputs],
        out_specs=[HBM if name == "finish" else VMEM] * len(shapes),
        scratch_shapes=list(scratch),
        cost_estimate=pl.CostEstimate(flops=int(flops * weight), bytes_accessed=int(moved * weight), transcendentals=0),
        compiler_params=pltpu.CompilerParams(vmem_limit_bytes=SOME_VMEM),
    )(*inputs)


def body(vectors_in, poles_one, roots_one, order_one, deflate_one, poles_two, roots_two, order_two, deflate_two):
    row_total = lax.axis_size("row")
    assert lax.axis_size("col") == 4
    row_place = lax.axis_index("row")
    col_place = lax.axis_index("col")
    local_rows, share = vectors_in.shape
    leaf = 4 * share
    width_one = 2 * leaf
    width_two = 4 * leaf
    columns = width_two // 4
    per_leaf = row_total // 4
    assert per_leaf % 2 == 0
    leaf_number = row_place // per_leaf
    pair = leaf_number // 2
    side = leaf_number % 2
    place = jnp.stack([pair, side, col_place, row_place % 2]).astype(jnp.int32)
    roots_two, order_two, poles_two, deflate_two = (
        a.reshape(1, width_two) for a in (roots_two, order_two, poles_two, deflate_two)
    )

    def along_col(x, moves):
        return lax.ppermute(x, "col", moves)

    rows = jnp.concatenate([vectors_in[0:1], vectors_in[local_rows - 1 :]], axis=0)
    rows = jnp.concatenate([rows] + [along_col(rows, [(i, i ^ k) for i in range(4)]) for k in (1, 2, 3)], axis=1)
    far = along_col(vectors_in, [(0, 2), (1, 3), (2, 0), (3, 1)])
    near = along_col(vectors_in, [(0, 1), (1, 0), (2, 3), (3, 2)])

    first_row, last_row = rows[0:1], rows[1:2]
    start = 2 * pair * per_leaf
    edges = jnp.concatenate(
        [
            jnp.where(row_place == start + per_leaf - 1, last_row, 0.0),
            jnp.where(row_place == start + per_leaf, first_row, 0.0),
            jnp.where(row_place == 2 * per_leaf - 1, last_row, jnp.where(row_place == 2 * per_leaf, first_row, 0.0)),
            jnp.zeros((5, leaf), F32),
        ],
        axis=0,
    )
    step = 1
    while step < 2 * per_leaf:
        edges = edges + lax.ppermute(edges, "row", [(i, i ^ step) for i in range(row_total)])
        step *= 2

    blocks = width_one // LANES
    raw = [poles_one, roots_one, order_one, deflate_one, poles_two, roots_two, order_two, deflate_two]
    raw = [pltpu.with_memory_space_constraint(x, pltpu.HBM) for x in raw]
    one_cols, two_cols, roots_one, flags_one, roots_two, flags_two = call(
        perm_kernel, "orders",
        [((LANES, 2 * blocks), F32)] * 2
        + [((1, width_one), F32), ((1, width_one), jnp.int32), ((1, columns), F32), ((1, columns), jnp.int32)],
        [place, *raw],
        scratch=[pltpu.VMEM(x.shape, x.dtype) for x in raw] + [pltpu.SemaphoreType.DMA((len(raw),))],
    )
    (sums,) = call(
        norm_one_kernel, "norm_one", [((2, width_one), F32)],
        [place, edges, one_cols, roots_one], flops=10 * leaf * width_one,
        scratch=[pltpu.VMEM((2 * share // LANES, LANES, 8), F32)],
    )
    sums_there = lax.ppermute(sums, "row", [(i, i ^ 1) for i in range(row_total)])
    one_high, one_low = call(
        table_one_kernel, "table_one", [((leaf // 2, width_one), BF16)] * 2,
        [one_cols, roots_one], flops=10 * leaf * width_one,
    )
    (table_two,) = call(
        table_two_kernel, "table_two", [((width_one, columns), F32)],
        [place, two_cols, roots_two], flops=10 * width_one * columns,
    )
    (weights,) = call(
        weight_kernel, "weights", [((LANES, 2 * blocks + leaf // 2 // LANES), F32)],
        [place, sums, sums_there, edges, flags_one, one_cols, two_cols],
    )
    b_high, b_low, squares = call(
        scale_kernel, "scale", [((width_one, columns), BF16)] * 2 + [((1, columns), F32)],
        [weights, table_two], flops=10 * width_one * columns,
    )
    half_row = row_total // 2
    squares_far = lax.ppermute(squares, "row", [(i, (i + half_row) % row_total) for i in range(row_total)])
    own_mids, other_mids = [], []
    for part in range(2):
        pieces = PIECES[part]
        own = call(
            functools.partial(mid_kernel, part), "mid", [((share // pieces, columns), F32)] * pieces,
            [weights, one_high, one_low, b_high, b_low], flops=6 * share * width_one * columns,
        )
        own_mids.append(own)
        if part == 0:
            b_high, near, far, from_middle = lax.optimization_barrier((b_high, near, far, vectors_in))
            last_end = along_col(far, [(1, 0), (2, 3)])
            last_middle = along_col(from_middle, [(1, 2), (2, 1)])
        other_mids.append([lax.ppermute(x, "row", [(i, i ^ 1) for i in range(row_total)]) for x in own])
    (total,) = call(
        apply_kernel, "apply", [((local_rows, columns), F32)],
        [place, *own_mids[0], *other_mids[0], vectors_in, far], flops=6 * local_rows * 2 * share * columns,
    )
    token, last_end, last_middle, total = lax.optimization_barrier((squares[:, :LANES], last_end, last_middle, total))
    token = lax.ppermute(token, "row", [(i, i ^ 1) for i in range(row_total)])
    total, token = lax.optimization_barrier((total, token))
    (merged,) = call(
        finish_kernel, "finish", [((local_rows, columns), F32)],
        [place, near, last_end, last_middle, total, squares, squares_far, flags_two, *own_mids[1], *other_mids[1]],
        flops=6 * local_rows * 2 * share * columns,
        scratch=[pltpu.VMEM((local_rows, columns), F32), pltpu.SemaphoreType.DMA((columns // WIDTH,))],
    )
    return merged


def solution(mesh):
    placed = (P("row", "col"), P(), P(), P(), P(), P(), P(), P(), P())
    return jax.shard_map(body, mesh=mesh, in_specs=placed, out_specs=P("row", "col"), check_vma=False)
```

time: 57.3 us -> 52.7 us (0.920)
  the two profiles are of different devices: /device:TPU:0 before, /device:TPU:12 now
where the time goes in v2:
time: 52.7 us; the launch traced here: 52.2 us
  Pallas kernels  25.6 us (49%)
  starting transfers between devices  17.2 us (33%)
  waiting for transfers between devices  7.86 us (15%)
  local copies, waits for them, and re-layouts  0.8 us (2%)
    pallas_call x10, Pallas kernels, call(): pl.pallas_call(kernel, name=name, out_shape=shapes, in_specs=[SMEM if x.s...  25.6 us
    ppermute x7, starting transfers between devices, along_col(): return lax.ppermute(x, 'col', moves)  14 us
    ppermute x7, waiting for transfers between devices, along_col(): return lax.ppermute(x, 'col', moves)  6.58 us
    ppermute x2, starting transfers between devices, body(): lax.ppermute(edges, 'row', [(i, i ^ step) for i in range(row_total)])  1.53 us
    ppermute x2, waiting for transfers between devices, body(): lax.ppermute(edges, 'row', [(i, i ^ step) for i in range(row_total)])  1.27 us
    ppermute x3, starting transfers between devices, body(): lax.ppermute(x, 'row', [(i, i ^ 1) for i in range(row_total)])  1.12 us
  transfers between devices with their start and end apart: 14, of which 4 were waited for; matrix products, arithmetic and copies ran while one was open for 1% of the time, Pallas kernels for 43%

profile of v2, /device:TPU:12, one launch (start us, length us, event | category | flops | bytes accessed | tf_op | source)
XLA Modules:
  0.0 52.2 jit_solution(3595857304029411157)
XLA Ops:
  0.0 0.7 %fusion.1 = (f32[1,256]{1,0:T(1,128)S(1)}, f32[1,256]{1,0:T(1,128)S(1)}) fusion(f32[512,256]{1,0:T(8,128)} %mine.1), kind=kLoop, calls=%fused_computation.9 | loop fusion | bytes 4096 | tf_op jit(solution)/shard_map/slice | solution.py:308
  0.7 0.5 collective-permute-start
  1.2 2.6 %collective-permute-start.1 = (f32[2,256]{1,0:T(2,128)S(1)}, f32[2,256]{1,0:T(2,128)S(1)}, u32[]{:S(2)}, u32[]{:S(2)}) collective-permute-start(f32[2,256]{1,0:T(2,128)S(1)} %pad_maximum_fusion.1), channel_id=1, source_target_pairs={{0,2},{1,3},{2,0},{3,1},{4,6},{5,7},{6,4},{7,5},{8,10},{9,11},{10,... | collective-permute-start | bytes 6152 | tf_op jit(solution)/shard_map/ppermute | solution.py:306
  4.3 1.3 %collective-permute-start.6 = (f32[512,256]{1,0:T(8,128)}, f32[512,256]{1,0:T(8,128)S(1)}, u32[]{:S(2)}, u32[]{:S(2)}) collective-permute-start(f32[512,256]{1,0:T(8,128)} %mine.1), channel_id=1, source_target_pairs={{0,1},{1,0},{2,3},{3,2},{4,5},{5,4},{6,7},{7,6},{8,9},{9,8},{10,11... | collective-permute-start | bytes 1572872 | tf_op jit(solution)/shard_map/ppermute | solution.py:306
  5.6 2.1 %collective-permute-start.7 = (f32[512,256]{1,0:T(8,128)}, f32[512,256]{1,0:T(8,128)S(1)}, u32[]{:S(2)}, u32[]{:S(2)}) collective-permute-start(f32[512,256]{1,0:T(8,128)} %mine.1), channel_id=1, source_target_pairs={{0,2},{1,3},{2,0},{3,1},{4,6},{5,7},{6,4},{7,5},{8,10},{9,11},{10,... | collective-permute-start | bytes 1572872 | tf_op jit(solution)/shard_map/ppermute | solution.py:306
  8.1 2.2 %orders.1 = (f32[128,32]{1,0:T(8,128)S(1)}, f32[128,32]{1,0:T(8,128)S(1)}, f32[1,2048]{1,0:T(1,128)S(1)}, s32[1,2048]{1,0:T(1,128)S(1)}, f32[1,1024]{1,0:T(1,128)S(1)}, /*index=5*/s32[1,1024]{1,0:T(1,128)S(1)}) custom-call(s32[4]{0:T(128)S(1)} %pad_add_fusion.place, f32[2,2048]{1,0:T(2,128)} %refs_0_.1, f32[2,2048]{1,0:T(2,128)} %refs_1_.1, ...), custom_call_target="tpu_custom_call" | custom-call | bytes 18843200 | tf_op jit(solution)/shard_map/orders/pallas_call | solution.py:273
  10.3 1.5 %collective-permute-start.4 = (f32[8,1024]{1,0:T(8,128)S(1)}, f32[8,1024]{1,0:T(8,128)S(1)}, u32[]{:S(2)}, u32[]{:S(2)}) collective-permute-start(f32[8,1024]{1,0:T(8,128)S(1)} %fusion), channel_id=1, source_target_pairs={{0,8},{4,12},{8,0},{12,4},{16,24},{20,28},{24,16},{28,20},{1,9},{5... | collective-permute-start | bytes 98312 | tf_op jit(solution)/shard_map/ppermute | solution.py:326
  11.8 1.2 %table_one.1 = (bf16[512,2048]{1,0:T(8,128)(2,1)S(1)}, bf16[512,2048]{1,0:T(8,128)(2,1)S(1)}) custom-call(f32[128,32]{1,0:T(8,128)S(1)} %get-tuple-element.25.cols_ref.one_cols, f32[1,2048]{1,0:T(1,128)S(1)} %get-tuple-element.26.roots_ref), custom_call_target="tpu_custom_call" | custom-call | flops 2097152000 | bytes 421888000 | tf_op jit(solution)/shard_map/table_one/pallas_call | solution.py:273
  13.0 1.3 %collective-permute-done.4 = f32[8,1024]{1,0:T(8,128)S(1)} collective-permute-done((f32[8,1024]{1,0:T(8,128)S(1)}, f32[8,1024]{1,0:T(8,128)S(1)}, u32[]{:S(2)}, u32[]{:S(2)}) %collective-permute-start.4) | collective-permute-done | bytes 32800 | tf_op jit(solution)/shard_map/ppermute | solution.py:326
  14.3 4.2 %norm_one.1.here = f32[2,2048]{1,0:T(2,128)S(1)} custom-call(s32[4]{0:T(128)S(1)} %pad_add_fusion.place, f32[8,1024]{1,0:T(8,128)S(1)} %fusion.2.edge_ref, f32[128,32]{1,0:T(8,128)S(1)} %get-tuple-element.25.cols_ref.one_cols, f32[1,2048]{1,0:T(1,128)S(1)} %get-tuple-element.26.roots_ref), custom_call_target="tpu_custom_call" | custom-call | flops 2097152000 | bytes 7374400 | tf_op jit(solution)/shard_map/norm_one/pallas_call | solution.py:273
  18.6 2.1 %table_two.1.two_ref = f32[2048,1024]{1,0:T(8,128)S(1)} custom-call(s32[4]{0:T(128)S(1)} %pad_add_fusion.place, f32[128,32]{1,0:T(8,128)S(1)} %get-tuple-element.28.two_cols.cols_ref, f32[1,1024]{1,0:T(1,128)S(1)} %get-tuple-element.29.roots_ref), custom_call_target="tpu_custom_call" | custom-call | flops 2097152000 | bytes 840910400 | tf_op jit(solution)/shard_map/table_two/pallas_call | solution.py:273
  20.7 0.8 %weights.1 = f32[128,36]{1,0:T(8,128)S(1)} custom-call(s32[4]{0:T(128)S(1)} %pad_add_fusion.place, f32[2,2048]{1,0:T(2,128)S(1)} %norm_one.1.here, f32[2,2048]{1,0:T(2,128)S(1)} %collective-permute-done.5.there, f32[8,1024]{1,0:T(8,128)S(1)} %fusion.2.edge_ref, s32[1,2048]{1,0:T(1,128)S(1)} %get-tuple-element.27.flags_ref, ...), custom_call_target="tpu_custom_call" | custom-call | bytes 124944 | tf_op jit(solution)/shard_map/weights/pallas_call | solution.py:273
  21.5 2.4 %scale.1 = (bf16[2048,1024]{1,0:T(8,128)(2,1)S(1)}, bf16[2048,1024]{1,0:T(8,128)(2,1)S(1)}, f32[1,1024]{1,0:T(1,128)S(1)}) custom-call(f32[128,36]{1,0:T(8,128)S(1)} %weights.1, f32[2048,1024]{1,0:T(8,128)S(1)} %table_two.1.two_ref), custom_call_target="tpu_custom_call" | custom-call | flops 20971520 | bytes 16799744 | tf_op jit(solution)/shard_map/scale/pallas_call | solution.py:273
  24.0 3.6 %mid.2.own_mid = f32[256,1024]{1,0:T(8,128)S(1)} custom-call(f32[128,36]{1,0:T(8,128)S(1)} %weights.1, bf16[512,2048]{1,0:T(8,128)(2,1)S(1)} %get-tuple-element.34.high_ref, bf16[512,2048]{1,0:T(8,128)(2,1)S(1)} %get-tuple-element.35.low_ref, bf16[2048,1024]{1,0:T(8,128)(2,1)S(1)} %get-tuple-element.42.b_high, bf16[2048,1024]{1,0:T(8,128)(2,1)S(1)} %get-tuple-element.36.b_low), custom_call_target="tpu_custom_call" | custom-call | flops 3221225472 | bytes 13649920 | tf_op jit(solution)/shard_map/mid/pallas_call | solution.py:273
  27.6 0.6 %collective-permute-start.10 = (f32[256,1024]{1,0:T(8,128)S(1)}, f32[256,1024]{1,0:T(8,128)S(1)}, u32[]{:S(2)}, u32[]{:S(2)}) collective-permute-start(f32[256,1024]{1,0:T(8,128)S(1)} %mid.2.own_mid), channel_id=1, source_target_pairs={{0,4},{4,0},{8,12},{12,8},{16,20},{20,16},{24,28},{28,24},{1,5},{5... | collective-permute-start | bytes 3145736 | tf_op jit(solution)/shard_map/ppermute | solution.py:375
  28.2 2.2 %collective-permute-done.7.far = f32[512,256]{1,0:T(8,128)S(1)} collective-permute-done((f32[512,256]{1,0:T(8,128)}, f32[512,256]{1,0:T(8,128)S(1)}, u32[]{:S(2)}, u32[]{:S(2)}) %collective-permute-start.7) | collective-permute-done | bytes 524320 | tf_op jit(solution)/shard_map/ppermute | solution.py:306
  30.4 3.6 %collective-permute-start.8 = (f32[512,256]{1,0:T(8,128)S(1)}, f32[512,256]{1,0:T(8,128)S(1)}, u32[]{:S(2)}, u32[]{:S(2)}) collective-permute-start(f32[512,256]{1,0:T(8,128)S(1)} %collective-permute-done.7.far), channel_id=1, source_target_pairs={{1,0},{2,3},{5,4},{6,7},{9,8},{10,11},{13,12},{14,15},{17,16},{18,... | collective-permute-start | bytes 1572872 | tf_op jit(solution)/shard_map/ppermute | solution.py:306
  34.0 3.4 %collective-permute-start.9 = (f32[512,256]{1,0:T(8,128)S(1)}, f32[512,256]{1,0:T(8,128)S(1)}, u32[]{:S(2)}, u32[]{:S(2)}) collective-permute-start(f32[512,256]{1,0:T(8,128)S(1)} %copy-done), channel_id=1, source_target_pairs={{1,2},{2,1},{5,6},{6,5},{9,10},{10,9},{13,14},{14,13},{17,18},{18,... | collective-permute-start | bytes 1572872 | tf_op jit(solution)/shard_map/ppermute | solution.py:306
  37.4 3.4 %mid.3 = (f32[128,1024]{1,0:T(8,128)S(1)}, f32[128,1024]{1,0:T(8,128)S(1)}) custom-call(f32[128,36]{1,0:T(8,128)S(1)} %weights.1, bf16[512,2048]{1,0:T(8,128)(2,1)S(1)} %get-tuple-element.34.high_ref, bf16[512,2048]{1,0:T(8,128)(2,1)S(1)} %get-tuple-element.35.low_ref, bf16[2048,1024]{1,0:T(8,128)(2,1)S(1)} %get-tuple-element.42.b_high, ...), custom_call_target="tpu_custom_call" | custom-call | flops 3221225472 | bytes 13649920 | tf_op jit(solution)/shard_map/mid/pallas_call | solution.py:273
  40.9 0.5 collective-permute-start.13
  41.4 0.5 collective-permute-start.11
  41.9 2.4 %apply.1.total_ref = f32[512,1024]{1,0:T(8,128)S(1)} custom-call(s32[4]{0:T(128)S(1)} %pad_add_fusion.place, f32[256,1024]{1,0:T(8,128)S(1)} %mid.2.own_mid, f32[256,1024]{1,0:T(8,128)S(1)} %collective-permute-done.10.other_mid, f32[512,256]{1,0:T(8,128)S(1)} %copy-done, f32[512,256]{1,0:T(8,128)S(1)} %collective-permute-done.7.far), custom_call_target="tpu_custom_call" | custom-call | flops 1610612 | bytes 5242 | tf_op jit(solution)/shard_map/apply/pallas_call | solution.py:273
  44.5 4.2 %collective-permute-done.9.last_middle = f32[512,256]{1,0:T(8,128)S(1)} collective-permute-done((f32[512,256]{1,0:T(8,128)S(1)}, f32[512,256]{1,0:T(8,128)S(1)}, u32[]{:S(2)}, u32[]{:S(2)}) %collective-permute-start.9) | collective-permute-done | bytes 524320 | tf_op jit(solution)/shard_map/ppermute | solution.py:306
  48.7 3.4 %finish.1 = f32[512,1024]{1,0:T(8,128)} custom-call(s32[4]{0:T(128)S(1)} %pad_add_fusion.place, f32[512,256]{1,0:T(8,128)S(1)} %collective-permute-done.6.near_ref, f32[512,256]{1,0:T(8,128)S(1)} %collective-permute-done.8.last_end, f32[512,256]{1,0:T(8,128)S(1)} %collective-permute-done.9.last_middle, f32[512,1024]{1,0:T(8,128)S(1)} %apply.1.total_ref, ...), custom_call_target="tpu_custom_call" | custom-call | flops 1610612 | bytes 7876 | tf_op jit(solution)/shard_map/finish/pallas_call | solution.py:273
  (26 shorter events, 1.2 us)
Async XLA Ops:
  0.7 7.1 %collective-permute-start = (f32[2,256]{1,0:T(2,128)S(1)}, f32[2,256]{1,0:T(2,128)S(1)}, u32[]{:S(2)}, u32[]{:S(2)}) collective-permute-start(f32[2,256]{1,0:T(2,128)S(1)} %pad_maximum_fusion.1), channel_id=1, source_target_pairs={{0,1},{1,0},{2,3},{3,2},{4,5},{5,4},{6,7},{7,6},{8,9},{9,8},{10,11... | collective-permute-start | bytes 6152 | tf_op jit(solution)/shard_map/ppermute | solution.py:306
  1.2 6.6 %collective-permute-start.1 = (f32[2,256]{1,0:T(2,128)S(1)}, f32[2,256]{1,0:T(2,128)S(1)}, u32[]{:S(2)}, u32[]{:S(2)}) collective-permute-start(f32[2,256]{1,0:T(2,128)S(1)} %pad_maximum_fusion.1), channel_id=1, source_target_pairs={{0,2},{1,3},{2,0},{3,1},{4,6},{5,7},{6,4},{7,5},{8,10},{9,11},{10,... | collective-permute-start | bytes 6152 | tf_op jit(solution)/shard_map/ppermute | solution.py:306
  3.8 4.0 %collective-permute-start.2 = (f32[2,256]{1,0:T(2,128)S(1)}, f32[2,256]{1,0:T(2,128)S(1)}, u32[]{:S(2)}, u32[]{:S(2)}) collective-permute-start(f32[2,256]{1,0:T(2,128)S(1)} %pad_maximum_fusion.1), channel_id=1, source_target_pairs={{0,3},{1,2},{2,1},{3,0},{4,7},{5,6},{6,5},{7,4},{8,11},{9,10},{10,... | collective-permute-start | bytes 6152 | tf_op jit(solution)/shard_map/ppermute | solution.py:306
  4.3 23.9 %collective-permute-start.6 = (f32[512,256]{1,0:T(8,128)}, f32[512,256]{1,0:T(8,128)S(1)}, u32[]{:S(2)}, u32[]{:S(2)}) collective-permute-start(f32[512,256]{1,0:T(8,128)} %mine.1), channel_id=1, source_target_pairs={{0,1},{1,0},{2,3},{3,2},{4,5},{5,4},{6,7},{7,6},{8,9},{9,8},{10,11... | collective-permute-start | bytes 1572872 | tf_op jit(solution)/shard_map/ppermute | solution.py:306
  5.6 24.8 %collective-permute-start.7 = (f32[512,256]{1,0:T(8,128)}, f32[512,256]{1,0:T(8,128)S(1)}, u32[]{:S(2)}, u32[]{:S(2)}) collective-permute-start(f32[512,256]{1,0:T(8,128)} %mine.1), channel_id=1, source_target_pairs={{0,2},{1,3},{2,0},{3,1},{4,6},{5,7},{6,4},{7,5},{8,10},{9,11},{10,... | collective-permute-start | bytes 1572872 | tf_op jit(solution)/shard_map/ppermute | solution.py:306
  8.0 2.3 %collective-permute-start.3 = (f32[8,1024]{1,0:T(8,128)S(1)}, f32[8,1024]{1,0:T(8,128)S(1)}, u32[]{:S(2)}, u32[]{:S(2)}) collective-permute-start(f32[8,1024]{1,0:T(8,128)S(1)} %maximum_maximum_fusion), channel_id=1, source_target_pairs={{0,4},{4,0},{8,12},{12,8},{16,20},{20,16},{24,28},{28,24},{1,5},{5... | collective-permute-start | bytes 98312 | tf_op jit(solution)/shard_map/ppermute | solution.py:326
  10.3 3.9 %collective-permute-start.4 = (f32[8,1024]{1,0:T(8,128)S(1)}, f32[8,1024]{1,0:T(8,128)S(1)}, u32[]{:S(2)}, u32[]{:S(2)}) collective-permute-start(f32[8,1024]{1,0:T(8,128)S(1)} %fusion), channel_id=1, source_target_pairs={{0,8},{4,12},{8,0},{12,4},{16,24},{20,28},{24,16},{28,20},{1,9},{5... | collective-permute-start | bytes 98312 | tf_op jit(solution)/shard_map/ppermute | solution.py:326
  18.5 2.2 %collective-permute-start.5 = (f32[2,2048]{1,0:T(2,128)S(1)}, f32[2,2048]{1,0:T(2,128)S(1)}, u32[]{:S(2)}, u32[]{:S(2)}) collective-permute-start(f32[2,2048]{1,0:T(2,128)S(1)} %norm_one.1.here), channel_id=1, source_target_pairs={{0,4},{4,0},{8,12},{12,8},{16,20},{20,16},{24,28},{28,24},{1,5},{5... | collective-permute-start | bytes 49160 | tf_op jit(solution)/shard_map/ppermute | solution.py:344
  24.0 10.1 %copy-start = (f32[512,256]{1,0:T(8,128)S(1)}, f32[512,256]{1,0:T(8,128)}, u32[]{:S(2)}) copy-start(f32[512,256]{1,0:T(8,128)} %mine.1) | copy-start | bytes 1572868
  27.6 13.8 %collective-permute-start.10 = (f32[256,1024]{1,0:T(8,128)S(1)}, f32[256,1024]{1,0:T(8,128)S(1)}, u32[]{:S(2)}, u32[]{:S(2)}) collective-permute-start(f32[256,1024]{1,0:T(8,128)S(1)} %mid.2.own_mid), channel_id=1, source_target_pairs={{0,4},{4,0},{8,12},{12,8},{16,20},{20,16},{24,28},{28,24},{1,5},{5... | collective-permute-start | bytes 3145736 | tf_op jit(solution)/shard_map/ppermute | solution.py:375
  30.4 14.1 %collective-permute-start.8 = (f32[512,256]{1,0:T(8,128)S(1)}, f32[512,256]{1,0:T(8,128)S(1)}, u32[]{:S(2)}, u32[]{:S(2)}) collective-permute-start(f32[512,256]{1,0:T(8,128)S(1)} %collective-permute-done.7.far), channel_id=1, source_target_pairs={{1,0},{2,3},{5,4},{6,7},{9,8},{10,11},{13,12},{14,15},{17,16},{18,... | collective-permute-start | bytes 1572872 | tf_op jit(solution)/shard_map/ppermute | solution.py:306
  34.0 14.6 %collective-permute-start.9 = (f32[512,256]{1,0:T(8,128)S(1)}, f32[512,256]{1,0:T(8,128)S(1)}, u32[]{:S(2)}, u32[]{:S(2)}) collective-permute-start(f32[512,256]{1,0:T(8,128)S(1)} %copy-done), channel_id=1, source_target_pairs={{1,2},{2,1},{5,6},{6,5},{9,10},{10,9},{13,14},{14,13},{17,18},{18,... | collective-permute-start | bytes 1572872 | tf_op jit(solution)/shard_map/ppermute | solution.py:306
  40.9 7.8 %collective-permute-start.12 = (f32[128,1024]{1,0:T(8,128)S(1)}, f32[128,1024]{1,0:T(8,128)S(1)}, u32[]{:S(2)}, u32[]{:S(2)}) collective-permute-start(f32[128,1024]{1,0:T(8,128)S(1)} %get-tuple-element.43.refs_0_), channel_id=1, source_target_pairs={{0,4},{4,0},{8,12},{12,8},{16,20},{20,16},{24,28},{28,24},{1,5},{5... | collective-permute-start | bytes 1572872 | tf_op jit(solution)/shard_map/ppermute | solution.py:375
  40.9 7.8 %collective-permute-start.13 = (f32[128,1024]{1,0:T(8,128)S(1)}, f32[128,1024]{1,0:T(8,128)S(1)}, u32[]{:S(2)}, u32[]{:S(2)}) collective-permute-start(f32[128,1024]{1,0:T(8,128)S(1)} %get-tuple-element.44.refs_1_), channel_id=1, source_target_pairs={{0,4},{4,0},{8,12},{12,8},{16,20},{20,16},{24,28},{28,24},{1,5},{5... | collective-permute-start | bytes 1572872 | tf_op jit(solution)/shard_map/ppermute | solution.py:375
  41.4 7.2 %collective-permute-start.11 = (f32[1,1024]{1,0:T(1,128)S(1)}, f32[1,1024]{1,0:T(1,128)S(1)}, u32[]{:S(2)}, u32[]{:S(2)}) collective-permute-start(f32[1,1024]{1,0:T(1,128)S(1)} %get-tuple-element.40.squares), channel_id=1, source_target_pairs={{0,16},{4,20},{8,24},{12,28},{16,0},{20,4},{24,8},{28,12},{1,17},{... | collective-permute-start | bytes 12296 | tf_op jit(solution)/shard_map/ppermute | solution.py:362

commit v3 on v2

--- a/solution.py
+++ b/solution.py
@@ -246,16 +246,16 @@
     scale = jnp.where(flags_ref[...] > 0, 1.0, lax.rsqrt(squares[...] + squares_far[...] + 1e-06))
     first = place[3] == 0
     near, last = near_ref[...], last_end[...] + last_middle[...]
-    own = split(jnp.where(first, near, last))
-    other = split(jnp.where(first, last, near))
+    own, other = jnp.where(first, near, last), jnp.where(first, last, near)
+    own_mid = split(jnp.concatenate([x[...] for x in own_late], axis=0))
+    other_mid = split(jnp.concatenate([x[...] for x in other_late], axis=0))
     copies = []
-    for i, at in enumerate(range(0, out_ref.shape[1], WIDTH)):
-        lanes = slice(at, at + WIDTH)
-        own_mid = jnp.concatenate([x[:, lanes] for x in own_late], axis=0)
-        other_mid = jnp.concatenate([x[:, lanes] for x in other_late], axis=0)
-        term = dot3(*own, *split(own_mid)) + dot3(*other, *split(other_mid))
-        done[:, lanes] = (total_ref[:, lanes] + term) * scale[:, lanes]
-        copies.append(pltpu.make_async_copy(done.at[:, lanes], out_ref.at[:, lanes], left.at[i]))
+    height = out_ref.shape[0] // left.shape[0]
+    for i in range(left.shape[0]):
+        rows = slice(height * i, height * (i + 1))
+        term = dot3(*split(own[rows]), *own_mid) + dot3(*split(other[rows]), *other_mid)
+        done[rows, :] = (total_ref[rows, :] + term) * scale
+        copies.append(pltpu.make_async_copy(done.at[rows, :], out_ref.at[rows, :], left.at[i]))
         copies[-1].start()
     for copy in copies:
         copy.wait()
@@ -264,6 +264,20 @@
 SMEM = pl.BlockSpec(memory_space=pltpu.SMEM)
 VMEM = pl.BlockSpec(memory_space=pltpu.VMEM)
 HBM = pl.BlockSpec(memory_space=pltpu.HBM)
+
+
+def coordinates():
+    per_leaf = lax.axis_size("row") // 4
+    row = lax.axis_index("row")
+    leaf = lax.div(row, jnp.int32(per_leaf))
+    return lax.div(leaf, jnp.int32(2)), lax.rem(leaf, jnp.int32(2)), lax.axis_index("col"), lax.rem(row, jnp.int32(2))
+
+
+def placed(kernel):
+    def run(*refs):
+        kernel(coordinates(), *refs)
+
+    return run
 
 
 def call(kernel, name, outs, inputs, flops=0, scratch=()):
@@ -337,8 +351,8 @@
         scratch=[pltpu.VMEM(x.shape, x.dtype) for x in raw] + [pltpu.SemaphoreType.DMA((len(raw),))],
     )
     (sums,) = call(
-        norm_one_kernel, "norm_one", [((2, width_one), F32)],
-        [place, edges, one_cols, roots_one], flops=10 * leaf * width_one,
+        placed(norm_one_kernel), "norm_one", [((2, width_one), F32)],
+        [edges, one_cols, roots_one], flops=10 * leaf * width_one,
         scratch=[pltpu.VMEM((2 * share // LANES, LANES, 8), F32)],
     )
     sums_there = lax.ppermute(sums, "row", [(i, i ^ 1) for i in range(row_total)])
@@ -347,12 +361,12 @@
         [one_cols, roots_one], flops=10 * leaf * width_one,
     )
     (table_two,) = call(
-        table_two_kernel, "table_two", [((width_one, columns), F32)],
-        [place, two_cols, roots_two], flops=10 * width_one * columns,
+        placed(table_two_kernel), "table_two", [((width_one, columns), F32)],
+        [two_cols, roots_two], flops=10 * width_one * columns,
     )
     (weights,) = call(
-        weight_kernel, "weights", [((LANES, 2 * blocks + leaf // 2 // LANES), F32)],
-        [place, sums, sums_there, edges, flags_one, one_cols, two_cols],
+        placed(weight_kernel), "weights", [((LANES, 2 * blocks + leaf // 2 // LANES), F32)],
+        [sums, sums_there, edges, flags_one, one_cols, two_cols],
     )
     b_high, b_low, squares = call(
         scale_kernel, "scale", [((width_one, columns), BF16)] * 2 + [((1, columns), F32)],
@@ -369,22 +383,22 @@
         )
         own_mids.append(own)
         if part == 0:
-            b_high, near, far, from_middle = lax.optimization_barrier((b_high, near, far, vectors_in))
+            b_high, near, far = lax.optimization_barrier((b_high, near, far))
             last_end = along_col(far, [(1, 0), (2, 3)])
-            last_middle = along_col(from_middle, [(1, 2), (2, 1)])
+            last_middle = along_col(vectors_in, [(1, 2), (2, 1)])
         other_mids.append([lax.ppermute(x, "row", [(i, i ^ 1) for i in range(row_total)]) for x in own])
     (total,) = call(
-        apply_kernel, "apply", [((local_rows, columns), F32)],
-        [place, *own_mids[0], *other_mids[0], vectors_in, far], flops=6 * local_rows * 2 * share * columns,
+        placed(apply_kernel), "apply", [((local_rows, columns), F32)],
+        [*own_mids[0], *other_mids[0], vectors_in, far], flops=6 * local_rows * 2 * share * columns,
     )
     token, last_end, last_middle, total = lax.optimization_barrier((squares[:, :LANES], last_end, last_middle, total))
     token = lax.ppermute(token, "row", [(i, i ^ 1) for i in range(row_total)])
     total, token = lax.optimization_barrier((total, token))
     (merged,) = call(
-        finish_kernel, "finish", [((local_rows, columns), F32)],
-        [place, near, last_end, last_middle, total, squares, squares_far, flags_two, *own_mids[1], *other_mids[1]],
+        placed(finish_kernel), "finish", [((local_rows, columns), F32)],
+        [near, last_end, last_middle, total, squares, squares_far, flags_two, *own_mids[1], *other_mids[1]],
         flops=6 * local_rows * 2 * share * columns,
-        scratch=[pltpu.VMEM((local_rows, columns), F32), pltpu.SemaphoreType.DMA((columns // WIDTH,))],
+        scratch=[pltpu.VMEM((local_rows, columns), F32), pltpu.SemaphoreType.DMA((4,))],
     )
     return merged
 

time: 52.7 us -> 50.5 us (0.958)
  the two profiles are of different devices: /device:TPU:12 before, /device:TPU:0 now
where the time goes in v3:
time: 50.5 us; the launch traced here: 50 us
  Pallas kernels  22.8 us (45%)
  starting transfers between devices  16.3 us (32%)
  waiting for transfers between devices  9.48 us (19%)
  local copies, waits for them, and re-layouts  0.8 us (2%)
    pallas_call x10, Pallas kernels, call(): pl.pallas_call(kernel, name=name, out_shape=shapes, in_specs=[SMEM if x.s...  22.8 us
    ppermute x7, starting transfers between devices, along_col(): return lax.ppermute(x, 'col', moves)  12 us
    ppermute x7, waiting for transfers between devices, along_col(): return lax.ppermute(x, 'col', moves)  8.19 us
    ppermute x2, starting transfers between devices, body(): lax.ppermute(edges, 'row', [(i, i ^ step) for i in range(row_total)])  1.53 us
    ppermute x1, starting transfers between devices, body(): lax.ppermute(squares, 'row', [(i, (i + half_row) % row_total) for i in ra...  1.52 us
    ppermute x2, waiting for transfers between devices, body(): lax.ppermute(edges, 'row', [(i, i ^ step) for i in range(row_total)])  1.27 us
    ppermute x3, starting transfers between devices, body(): lax.ppermute(x, 'row', [(i, i ^ 1) for i in range(row_total)])  1.13 us
  transfers between devices with their start and end apart: 14, of which 4 were waited for; matrix products, arithmetic and copies ran while one was open for 1% of the time, Pallas kernels for 40%

profile of v3, /device:TPU:0, one launch (start us, length us, event | category | flops | bytes accessed | tf_op | source)
XLA Modules:
  0.0 50.0 jit_solution(6359137815288499687)
XLA Ops:
  0.0 0.7 %fusion.1 = (f32[1,256]{1,0:T(1,128)S(1)}, f32[1,256]{1,0:T(1,128)S(1)}) fusion(f32[512,256]{1,0:T(8,128)} %refs_2_.3), kind=kLoop, calls=%fused_computation.9 | loop fusion | bytes 4096 | tf_op jit(solution)/shard_map/slice | solution.py:322
  0.7 3.1 %collective-permute-start = (f32[2,256]{1,0:T(2,128)S(1)}, f32[2,256]{1,0:T(2,128)S(1)}, u32[]{:S(2)}, u32[]{:S(2)}) collective-permute-start(f32[2,256]{1,0:T(2,128)S(1)} %pad_maximum_fusion.1), channel_id=1, source_target_pairs={{0,1},{1,0},{2,3},{3,2},{4,5},{5,4},{6,7},{7,6},{8,9},{9,8},{10,11... | collective-permute-start | bytes 6152 | tf_op jit(solution)/shard_map/ppermute | solution.py:320
  3.8 2.6 %collective-permute-start.1 = (f32[2,256]{1,0:T(2,128)S(1)}, f32[2,256]{1,0:T(2,128)S(1)}, u32[]{:S(2)}, u32[]{:S(2)}) collective-permute-start(f32[2,256]{1,0:T(2,128)S(1)} %pad_maximum_fusion.1), channel_id=1, source_target_pairs={{0,2},{1,3},{2,0},{3,1},{4,6},{5,7},{6,4},{7,5},{8,10},{9,11},{10,... | collective-permute-start | bytes 6152 | tf_op jit(solution)/shard_map/ppermute | solution.py:320
  6.4 0.9 %collective-permute-start.6 = (f32[512,256]{1,0:T(8,128)}, f32[512,256]{1,0:T(8,128)S(1)}, u32[]{:S(2)}, u32[]{:S(2)}) collective-permute-start(f32[512,256]{1,0:T(8,128)} %refs_2_.3), channel_id=1, source_target_pairs={{0,1},{1,0},{2,3},{3,2},{4,5},{5,4},{6,7},{7,6},{8,9},{9,8},{10,11... | collective-permute-start | bytes 1572872 | tf_op jit(solution)/shard_map/ppermute | solution.py:320
  7.3 3.5 %collective-permute-start.7 = (f32[512,256]{1,0:T(8,128)}, f32[512,256]{1,0:T(8,128)S(1)}, u32[]{:S(2)}, u32[]{:S(2)}) collective-permute-start(f32[512,256]{1,0:T(8,128)} %refs_2_.3), channel_id=1, source_target_pairs={{0,2},{1,3},{2,0},{3,1},{4,6},{5,7},{6,4},{7,5},{8,10},{9,11},{10,... | collective-permute-start | bytes 1572872 | tf_op jit(solution)/shard_map/ppermute | solution.py:320
  10.9 1.1 %collective-permute-done.2 = f32[2,256]{1,0:T(2,128)S(1)} collective-permute-done((f32[2,256]{1,0:T(2,128)S(1)}, f32[2,256]{1,0:T(2,128)S(1)}, u32[]{:S(2)}, u32[]{:S(2)}) %collective-permute-start.2) | collective-permute-done | bytes 2080 | tf_op jit(solution)/shard_map/ppermute | solution.py:320
  12.2 2.2 %orders.1 = (f32[128,32]{1,0:T(8,128)S(1)}, f32[128,32]{1,0:T(8,128)S(1)}, f32[1,2048]{1,0:T(1,128)S(1)}, s32[1,2048]{1,0:T(1,128)S(1)}, f32[1,1024]{1,0:T(1,128)S(1)}, /*index=5*/s32[1,1024]{1,0:T(1,128)S(1)}) custom-call(s32[4]{0:T(128)S(1)} %pad_add_fusion.place, f32[2,2048]{1,0:T(2,128)} %refs_0_.1, f32[2,2048]{1,0:T(2,128)} %refs_1_.1, ...), custom_call_target="tpu_custom_call" | custom-call | bytes 18843200 | tf_op jit(solution)/shard_map/orders/pallas_call | solution.py:287
  14.4 1.5 %collective-permute-start.4 = (f32[8,1024]{1,0:T(8,128)S(1)}, f32[8,1024]{1,0:T(8,128)S(1)}, u32[]{:S(2)}, u32[]{:S(2)}) collective-permute-start(f32[8,1024]{1,0:T(8,128)S(1)} %fusion), channel_id=1, source_target_pairs={{0,8},{4,12},{8,0},{12,4},{16,24},{20,28},{24,16},{28,20},{1,9},{5... | collective-permute-start | bytes 98312 | tf_op jit(solution)/shard_map/ppermute | solution.py:340
  15.9 1.1 %table_one.1 = (bf16[512,2048]{1,0:T(8,128)(2,1)S(1)}, bf16[512,2048]{1,0:T(8,128)(2,1)S(1)}) custom-call(f32[128,32]{1,0:T(8,128)S(1)} %get-tuple-element.24.refs_1_.refs_4_.cols_ref, f32[1,2048]{1,0:T(1,128)S(1)} %get-tuple-element.25.refs_2_.roots_ref), custom_call_target="tpu_custom_call" | custom-call | flops 2097152000 | bytes 421888000 | tf_op jit(solution)/shard_map/table_one/pallas_call | solution.py:287
  17.1 1.3 %collective-permute-done.4 = f32[8,1024]{1,0:T(8,128)S(1)} collective-permute-done((f32[8,1024]{1,0:T(8,128)S(1)}, f32[8,1024]{1,0:T(8,128)S(1)}, u32[]{:S(2)}, u32[]{:S(2)}) %collective-permute-start.4) | collective-permute-done | bytes 32800 | tf_op jit(solution)/shard_map/ppermute | solution.py:340
  18.4 3.6 %norm_one.1.refs_0_ = f32[2,2048]{1,0:T(2,128)S(1)} custom-call(f32[8,1024]{1,0:T(8,128)S(1)} %fusion.2.refs_0_.refs_2_, f32[128,32]{1,0:T(8,128)S(1)} %get-tuple-element.24.refs_1_.refs_4_.cols_ref, f32[1,2048]{1,0:T(1,128)S(1)} %get-tuple-element.25.refs_2_.roots_ref), custom_call_target="tpu_custom_call" | custom-call | flops 2097152000 | bytes 7372800 | tf_op jit(solution)/shard_map/norm_one/pallas_call | solution.py:287
  22.1 1.6 %table_two.1.two_ref = f32[2048,1024]{1,0:T(8,128)S(1)} custom-call(f32[128,32]{1,0:T(8,128)S(1)} %get-tuple-element.27.refs_5_.refs_0_, f32[1,1024]{1,0:T(1,128)S(1)} %get-tuple-element.28.refs_1_), custom_call_target="tpu_custom_call" | custom-call | flops 2097152000 | bytes 840908800 | tf_op jit(solution)/shard_map/table_two/pallas_call | solution.py:287
  24.0 2.4 %scale.1 = (bf16[2048,1024]{1,0:T(8,128)(2,1)S(1)}, bf16[2048,1024]{1,0:T(8,128)(2,1)S(1)}, f32[1,1024]{1,0:T(1,128)S(1)}) custom-call(f32[128,36]{1,0:T(8,128)S(1)} %weights.1, f32[2048,1024]{1,0:T(8,128)S(1)} %table_two.1.two_ref), custom_call_target="tpu_custom_call" | custom-call | flops 20971520 | bytes 16799744 | tf_op jit(solution)/shard_map/scale/pallas_call | solution.py:287
  26.4 3.6 %mid.2.refs_0_ = f32[256,1024]{1,0:T(8,128)S(1)} custom-call(f32[128,36]{1,0:T(8,128)S(1)} %weights.1, bf16[512,2048]{1,0:T(8,128)(2,1)S(1)} %get-tuple-element.32.high_ref, bf16[512,2048]{1,0:T(8,128)(2,1)S(1)} %get-tuple-element.33.low_ref, bf16[2048,1024]{1,0:T(8,128)(2,1)S(1)} %get-tuple-element.40.b_high, bf16[2048,1024]{1,0:T(8,128)(2,1)S(1)} %get-tuple-element.34.b_low), custom_call_target="tpu_custom_call" | custom-call | flops 3221225472 | bytes 13649920 | tf_op jit(solution)/shard_map/mid/pallas_call | solution.py:287
  30.0 0.6 %collective-permute-start.10 = (f32[256,1024]{1,0:T(8,128)S(1)}, f32[256,1024]{1,0:T(8,128)S(1)}, u32[]{:S(2)}, u32[]{:S(2)}) collective-permute-start(f32[256,1024]{1,0:T(8,128)S(1)} %mid.2.refs_0_), channel_id=1, source_target_pairs={{0,4},{4,0},{8,12},{12,8},{16,20},{20,16},{24,28},{28,24},{1,5},{5... | collective-permute-start | bytes 3145736 | tf_op jit(solution)/shard_map/ppermute | solution.py:389
  30.6 0.7 %collective-permute-start.9 = (f32[512,256]{1,0:T(8,128)S(1)}, f32[512,256]{1,0:T(8,128)S(1)}, u32[]{:S(2)}, u32[]{:S(2)}) collective-permute-start(f32[512,256]{1,0:T(8,128)S(1)} %copy-done), channel_id=1, source_target_pairs={{1,2},{2,1},{5,6},{6,5},{9,10},{10,9},{13,14},{14,13},{17,18},{18,... | collective-permute-start | bytes 1572872 | tf_op jit(solution)/shard_map/ppermute | solution.py:320
  31.3 1.8 %collective-permute-done.7.refs_3_ = f32[512,256]{1,0:T(8,128)S(1)} collective-permute-done((f32[512,256]{1,0:T(8,128)}, f32[512,256]{1,0:T(8,128)S(1)}, u32[]{:S(2)}, u32[]{:S(2)}) %collective-permute-start.7) | collective-permute-done | bytes 524320 | tf_op jit(solution)/shard_map/ppermute | solution.py:320
  33.1 1.3 %collective-permute-start.8 = (f32[512,256]{1,0:T(8,128)S(1)}, f32[512,256]{1,0:T(8,128)S(1)}, u32[]{:S(2)}, u32[]{:S(2)}) collective-permute-start(f32[512,256]{1,0:T(8,128)S(1)} %collective-permute-done.7.refs_3_), channel_id=1, source_target_pairs={{1,0},{2,3},{5,4},{6,7},{9,8},{10,11},{13,12},{14,15},{17,16},{18,... | collective-permute-start | bytes 1572872 | tf_op jit(solution)/shard_map/ppermute | solution.py:320
  34.4 3.4 %mid.3 = (f32[128,1024]{1,0:T(8,128)S(1)}, f32[128,1024]{1,0:T(8,128)S(1)}) custom-call(f32[128,36]{1,0:T(8,128)S(1)} %weights.1, bf16[512,2048]{1,0:T(8,128)(2,1)S(1)} %get-tuple-element.32.high_ref, bf16[512,2048]{1,0:T(8,128)(2,1)S(1)} %get-tuple-element.33.low_ref, bf16[2048,1024]{1,0:T(8,128)(2,1)S(1)} %get-tuple-element.40.b_high, ...), custom_call_target="tpu_custom_call" | custom-call | flops 3221225472 | bytes 13649920 | tf_op jit(solution)/shard_map/mid/pallas_call | solution.py:287
  37.9 0.5 collective-permute-start.13
  38.4 1.5 %collective-permute-start.11 = (f32[1,1024]{1,0:T(1,128)S(1)}, f32[1,1024]{1,0:T(1,128)S(1)}, u32[]{:S(2)}, u32[]{:S(2)}) collective-permute-start(f32[1,1024]{1,0:T(1,128)S(1)} %get-tuple-element.38.refs_4_), channel_id=1, source_target_pairs={{0,16},{4,20},{8,24},{12,28},{16,0},{20,4},{24,8},{28,12},{1,17},{... | collective-permute-start | bytes 12296 | tf_op jit(solution)/shard_map/ppermute | solution.py:376
  39.9 1.8 %apply.1.refs_3_ = f32[512,1024]{1,0:T(8,128)S(1)} custom-call(f32[256,1024]{1,0:T(8,128)S(1)} %mid.2.refs_0_, f32[256,1024]{1,0:T(8,128)S(1)} %collective-permute-done.10.refs_1_, f32[512,256]{1,0:T(8,128)S(1)} %copy-done, f32[512,256]{1,0:T(8,128)S(1)} %collective-permute-done.7.refs_3_), custom_call_target="tpu_custom_call" | custom-call | flops 1610612 | bytes 5242 | tf_op jit(solution)/shard_map/apply/pallas_call | solution.py:287
  41.7 5.3 %collective-permute-done.8.refs_1_ = f32[512,256]{1,0:T(8,128)S(1)} collective-permute-done((f32[512,256]{1,0:T(8,128)S(1)}, f32[512,256]{1,0:T(8,128)S(1)}, u32[]{:S(2)}, u32[]{:S(2)}) %collective-permute-start.8) | collective-permute-done | bytes 524320 | tf_op jit(solution)/shard_map/ppermute | solution.py:320
  47.1 2.8 %finish.1 = f32[512,1024]{1,0:T(8,128)} custom-call(f32[512,256]{1,0:T(8,128)S(1)} %collective-permute-done.6.refs_0_, f32[512,256]{1,0:T(8,128)S(1)} %collective-permute-done.8.refs_1_, f32[512,256]{1,0:T(8,128)S(1)} %collective-permute-done.9.refs_2_, f32[512,1024]{1,0:T(8,128)S(1)} %apply.1.refs_3_, f32[1,1024]{1,0:T(1,128)S(1)} %get-tuple-element.38.refs_4_, ...), custom_call_target="tpu_custom_call" | custom-call | flops 1610612 | bytes 7876 | tf_op jit(solution)/shard_map/finish/pallas_call | solution.py:287
  (26 shorter events, 0.9 us)
Async XLA Ops:
  0.7 10.1 %collective-permute-start = (f32[2,256]{1,0:T(2,128)S(1)}, f32[2,256]{1,0:T(2,128)S(1)}, u32[]{:S(2)}, u32[]{:S(2)}) collective-permute-start(f32[2,256]{1,0:T(2,128)S(1)} %pad_maximum_fusion.1), channel_id=1, source_target_pairs={{0,1},{1,0},{2,3},{3,2},{4,5},{5,4},{6,7},{7,6},{8,9},{9,8},{10,11... | collective-permute-start | bytes 6152 | tf_op jit(solution)/shard_map/ppermute | solution.py:320
  3.8 7.1 %collective-permute-start.1 = (f32[2,256]{1,0:T(2,128)S(1)}, f32[2,256]{1,0:T(2,128)S(1)}, u32[]{:S(2)}, u32[]{:S(2)}) collective-permute-start(f32[2,256]{1,0:T(2,128)S(1)} %pad_maximum_fusion.1), channel_id=1, source_target_pairs={{0,2},{1,3},{2,0},{3,1},{4,6},{5,7},{6,4},{7,5},{8,10},{9,11},{10,... | collective-permute-start | bytes 6152 | tf_op jit(solution)/shard_map/ppermute | solution.py:320
  6.4 5.5 %collective-permute-start.2 = (f32[2,256]{1,0:T(2,128)S(1)}, f32[2,256]{1,0:T(2,128)S(1)}, u32[]{:S(2)}, u32[]{:S(2)}) collective-permute-start(f32[2,256]{1,0:T(2,128)S(1)} %pad_maximum_fusion.1), channel_id=1, source_target_pairs={{0,3},{1,2},{2,1},{3,0},{4,7},{5,6},{6,5},{7,4},{8,11},{9,10},{10,... | collective-permute-start | bytes 6152 | tf_op jit(solution)/shard_map/ppermute | solution.py:320
  6.4 24.9 %collective-permute-start.6 = (f32[512,256]{1,0:T(8,128)}, f32[512,256]{1,0:T(8,128)S(1)}, u32[]{:S(2)}, u32[]{:S(2)}) collective-permute-start(f32[512,256]{1,0:T(8,128)} %refs_2_.3), channel_id=1, source_target_pairs={{0,1},{1,0},{2,3},{3,2},{4,5},{5,4},{6,7},{7,6},{8,9},{9,8},{10,11... | collective-permute-start | bytes 1572872 | tf_op jit(solution)/shard_map/ppermute | solution.py:320
  7.3 25.8 %collective-permute-start.7 = (f32[512,256]{1,0:T(8,128)}, f32[512,256]{1,0:T(8,128)S(1)}, u32[]{:S(2)}, u32[]{:S(2)}) collective-permute-start(f32[512,256]{1,0:T(8,128)} %refs_2_.3), channel_id=1, source_target_pairs={{0,2},{1,3},{2,0},{3,1},{4,6},{5,7},{6,4},{7,5},{8,10},{9,11},{10,... | collective-permute-start | bytes 1572872 | tf_op jit(solution)/shard_map/ppermute | solution.py:320
  12.0 2.3 %collective-permute-start.3 = (f32[8,1024]{1,0:T(8,128)S(1)}, f32[8,1024]{1,0:T(8,128)S(1)}, u32[]{:S(2)}, u32[]{:S(2)}) collective-permute-start(f32[8,1024]{1,0:T(8,128)S(1)} %maximum_maximum_fusion), channel_id=1, source_target_pairs={{0,4},{4,0},{8,12},{12,8},{16,20},{20,16},{24,28},{28,24},{1,5},{5... | collective-permute-start | bytes 98312 | tf_op jit(solution)/shard_map/ppermute | solution.py:340
  14.4 3.9 %collective-permute-start.4 = (f32[8,1024]{1,0:T(8,128)S(1)}, f32[8,1024]{1,0:T(8,128)S(1)}, u32[]{:S(2)}, u32[]{:S(2)}) collective-permute-start(f32[8,1024]{1,0:T(8,128)S(1)} %fusion), channel_id=1, source_target_pairs={{0,8},{4,12},{8,0},{12,4},{16,24},{20,28},{24,16},{28,20},{1,9},{5... | collective-permute-start | bytes 98312 | tf_op jit(solution)/shard_map/ppermute | solution.py:340
  22.0 1.6 %collective-permute-start.5 = (f32[2,2048]{1,0:T(2,128)S(1)}, f32[2,2048]{1,0:T(2,128)S(1)}, u32[]{:S(2)}, u32[]{:S(2)}) collective-permute-start(f32[2,2048]{1,0:T(2,128)S(1)} %norm_one.1.refs_0_), channel_id=1, source_target_pairs={{0,4},{4,0},{8,12},{12,8},{16,20},{20,16},{24,28},{28,24},{1,5},{5... | collective-permute-start | bytes 49160 | tf_op jit(solution)/shard_map/ppermute | solution.py:358
  26.4 4.2 %copy-start = (f32[512,256]{1,0:T(8,128)S(1)}, f32[512,256]{1,0:T(8,128)}, u32[]{:S(2)}) copy-start(f32[512,256]{1,0:T(8,128)} %refs_2_.3) | copy-start | bytes 1572868
  30.0 8.4 %collective-permute-start.10 = (f32[256,1024]{1,0:T(8,128)S(1)}, f32[256,1024]{1,0:T(8,128)S(1)}, u32[]{:S(2)}, u32[]{:S(2)}) collective-permute-start(f32[256,1024]{1,0:T(8,128)S(1)} %mid.2.refs_0_), channel_id=1, source_target_pairs={{0,4},{4,0},{8,12},{12,8},{16,20},{20,16},{24,28},{28,24},{1,5},{5... | collective-permute-start | bytes 3145736 | tf_op jit(solution)/shard_map/ppermute | solution.py:389
  30.6 11.1 %collective-permute-start.9 = (f32[512,256]{1,0:T(8,128)S(1)}, f32[512,256]{1,0:T(8,128)S(1)}, u32[]{:S(2)}, u32[]{:S(2)}) collective-permute-start(f32[512,256]{1,0:T(8,128)S(1)} %copy-done), channel_id=1, source_target_pairs={{1,2},{2,1},{5,6},{6,5},{9,10},{10,9},{13,14},{14,13},{17,18},{18,... | collective-permute-start | bytes 1572872 | tf_op jit(solution)/shard_map/ppermute | solution.py:320
  33.1 14.0 %collective-permute-start.8 = (f32[512,256]{1,0:T(8,128)S(1)}, f32[512,256]{1,0:T(8,128)S(1)}, u32[]{:S(2)}, u32[]{:S(2)}) collective-permute-start(f32[512,256]{1,0:T(8,128)S(1)} %collective-permute-done.7.refs_3_), channel_id=1, source_target_pairs={{1,0},{2,3},{5,4},{6,7},{9,8},{10,11},{13,12},{14,15},{17,16},{18,... | collective-permute-start | bytes 1572872 | tf_op jit(solution)/shard_map/ppermute | solution.py:320
  37.8 9.3 %collective-permute-start.12 = (f32[128,1024]{1,0:T(8,128)S(1)}, f32[128,1024]{1,0:T(8,128)S(1)}, u32[]{:S(2)}, u32[]{:S(2)}) collective-permute-start(f32[128,1024]{1,0:T(8,128)S(1)} %get-tuple-element.41.refs_7_), channel_id=1, source_target_pairs={{0,4},{4,0},{8,12},{12,8},{16,20},{20,16},{24,28},{28,24},{1,5},{5... | collective-permute-start | bytes 1572872 | tf_op jit(solution)/shard_map/ppermute | solution.py:389
  37.9 9.2 %collective-permute-start.13 = (f32[128,1024]{1,0:T(8,128)S(1)}, f32[128,1024]{1,0:T(8,128)S(1)}, u32[]{:S(2)}, u32[]{:S(2)}) collective-permute-start(f32[128,1024]{1,0:T(8,128)S(1)} %get-tuple-element.42.refs_8_), channel_id=1, source_target_pairs={{0,4},{4,0},{8,12},{12,8},{16,20},{20,16},{24,28},{28,24},{1,5},{5... | collective-permute-start | bytes 1572872 | tf_op jit(solution)/shard_map/ppermute | solution.py:389
  38.4 8.7 %collective-permute-start.11 = (f32[1,1024]{1,0:T(1,128)S(1)}, f32[1,1024]{1,0:T(1,128)S(1)}, u32[]{:S(2)}, u32[]{:S(2)}) collective-permute-start(f32[1,1024]{1,0:T(1,128)S(1)} %get-tuple-element.38.refs_4_), channel_id=1, source_target_pairs={{0,16},{4,20},{8,24},{12,28},{16,0},{20,4},{24,8},{28,12},{1,17},{... | collective-permute-start | bytes 12296 | tf_op jit(solution)/shard_map/ppermute | solution.py:376

commit v4 on v3

--- a/solution.py
+++ b/solution.py
@@ -14,7 +14,7 @@
 SOME_VMEM = 14 * 1024 * 1024
 ROWS, WIDTH = 32, 512
 PIECES = (1, 2)
-WEIGHTS = {"orders": 100, "table_one": 100, "table_two": 100, "norm_one": 100, "apply": 0.001, "finish": 0.001}
+WEIGHTS = {"orders": 100, "table_one": 100, "table_two": 100, "norm_one": 100, "apply": 0.001, "mid_late": 6, "finish": 0.001}
 
 
 def split(x):
@@ -378,7 +378,7 @@
     for part in range(2):
         pieces = PIECES[part]
         own = call(
-            functools.partial(mid_kernel, part), "mid", [((share // pieces, columns), F32)] * pieces,
+            functools.partial(mid_kernel, part), ("mid", "mid_late")[part], [((share // pieces, columns), F32)] * pieces,
             [weights, one_high, one_low, b_high, b_low], flops=6 * share * width_one * columns,
         )
         own_mids.append(own)

time: 50.5 us -> 49.9 us (0.988)
  waiting for transfers between devices: 9.48 us -> 8.89 us
    ppermute x7, waiting for transfers between devices: 8.19 us -> 7.61 us  [along_col(): return lax.ppermute(x, 'col', moves)]
  transfers between devices with their start and end apart: 14 -> 14, of which waited for: 4 -> 4; matrix products, arithmetic and copies ran while one was open for 1% -> 1% of each run, Pallas kernels for 40% -> 41%
where the time goes in v4:
time: 49.9 us; the launch traced here: 49.4 us
  Pallas kernels  22.8 us (46%)
  starting transfers between devices  16.3 us (33%)
  waiting for transfers between devices  8.89 us (18%)
  local copies, waits for them, and re-layouts  0.8 us (2%)
    pallas_call x10, Pallas kernels, call(): pl.pallas_call(kernel, name=name, out_shape=shapes, in_specs=[SMEM if x.s...  22.8 us
    ppermute x7, starting transfers between devices, along_col(): return lax.ppermute(x, 'col', moves)  12 us
    ppermute x7, waiting for transfers between devices, along_col(): return lax.ppermute(x, 'col', moves)  7.61 us
    ppermute x2, starting transfers between devices, body(): lax.ppermute(edges, 'row', [(i, i ^ step) for i in range(row_total)])  1.53 us
    ppermute x1, starting transfers between devices, body(): lax.ppermute(squares, 'row', [(i, (i + half_row) % row_total) for i in ra...  1.52 us
    ppermute x2, waiting for transfers between devices, body(): lax.ppermute(edges, 'row', [(i, i ^ step) for i in range(row_total)])  1.27 us
    ppermute x3, starting transfers between devices, body(): lax.ppermute(x, 'row', [(i, i ^ 1) for i in range(row_total)])  1.13 us
  transfers between devices with their start and end apart: 14, of which 4 were waited for; matrix products, arithmetic and copies ran while one was open for 1% of the time, Pallas kernels for 41%

profile of v4, /device:TPU:0, one launch (start us, length us, event | category | flops | bytes accessed | tf_op | source)
XLA Modules:
  0.0 49.4 jit_solution(18247894676852166935)
XLA Ops:
  0.0 0.7 %fusion.1 = (f32[1,256]{1,0:T(1,128)S(1)}, f32[1,256]{1,0:T(1,128)S(1)}) fusion(f32[512,256]{1,0:T(8,128)} %refs_2_.3), kind=kLoop, calls=%fused_computation.9 | loop fusion | bytes 4096 | tf_op jit(solution)/shard_map/slice | solution.py:322
  0.7 3.1 %collective-permute-start = (f32[2,256]{1,0:T(2,128)S(1)}, f32[2,256]{1,0:T(2,128)S(1)}, u32[]{:S(2)}, u32[]{:S(2)}) collective-permute-start(f32[2,256]{1,0:T(2,128)S(1)} %pad_maximum_fusion.1), channel_id=1, source_target_pairs={{0,1},{1,0},{2,3},{3,2},{4,5},{5,4},{6,7},{7,6},{8,9},{9,8},{10,11... | collective-permute-start | bytes 6152 | tf_op jit(solution)/shard_map/ppermute | solution.py:320
  3.8 2.6 %collective-permute-start.1 = (f32[2,256]{1,0:T(2,128)S(1)}, f32[2,256]{1,0:T(2,128)S(1)}, u32[]{:S(2)}, u32[]{:S(2)}) collective-permute-start(f32[2,256]{1,0:T(2,128)S(1)} %pad_maximum_fusion.1), channel_id=1, source_target_pairs={{0,2},{1,3},{2,0},{3,1},{4,6},{5,7},{6,4},{7,5},{8,10},{9,11},{10,... | collective-permute-start | bytes 6152 | tf_op jit(solution)/shard_map/ppermute | solution.py:320
  6.4 0.9 %collective-permute-start.6 = (f32[512,256]{1,0:T(8,128)}, f32[512,256]{1,0:T(8,128)S(1)}, u32[]{:S(2)}, u32[]{:S(2)}) collective-permute-start(f32[512,256]{1,0:T(8,128)} %refs_2_.3), channel_id=1, source_target_pairs={{0,1},{1,0},{2,3},{3,2},{4,5},{5,4},{6,7},{7,6},{8,9},{9,8},{10,11... | collective-permute-start | bytes 1572872 | tf_op jit(solution)/shard_map/ppermute | solution.py:320
  7.3 3.5 %collective-permute-start.7 = (f32[512,256]{1,0:T(8,128)}, f32[512,256]{1,0:T(8,128)S(1)}, u32[]{:S(2)}, u32[]{:S(2)}) collective-permute-start(f32[512,256]{1,0:T(8,128)} %refs_2_.3), channel_id=1, source_target_pairs={{0,2},{1,3},{2,0},{3,1},{4,6},{5,7},{6,4},{7,5},{8,10},{9,11},{10,... | collective-permute-start | bytes 1572872 | tf_op jit(solution)/shard_map/ppermute | solution.py:320
  10.9 0.7 %collective-permute-start.9 = (f32[512,256]{1,0:T(8,128)}, f32[512,256]{1,0:T(8,128)S(1)}, u32[]{:S(2)}, u32[]{:S(2)}) collective-permute-start(f32[512,256]{1,0:T(8,128)} %refs_2_.3), channel_id=1, source_target_pairs={{1,2},{2,1},{5,6},{6,5},{9,10},{10,9},{13,14},{14,13},{17,18},{18,... | collective-permute-start | bytes 1572872 | tf_op jit(solution)/shard_map/ppermute | solution.py:320
  11.6 0.4 collective-permute-done.2
  12.2 2.2 %orders.1 = (f32[128,32]{1,0:T(8,128)S(1)}, f32[128,32]{1,0:T(8,128)S(1)}, f32[1,2048]{1,0:T(1,128)S(1)}, s32[1,2048]{1,0:T(1,128)S(1)}, f32[1,1024]{1,0:T(1,128)S(1)}, /*index=5*/s32[1,1024]{1,0:T(1,128)S(1)}) custom-call(s32[4]{0:T(128)S(1)} %pad_add_fusion.place, f32[2,2048]{1,0:T(2,128)} %refs_0_.1, f32[2,2048]{1,0:T(2,128)} %refs_1_.1, ...), custom_call_target="tpu_custom_call" | custom-call | bytes 18843200 | tf_op jit(solution)/shard_map/orders/pallas_call | solution.py:287
  14.4 1.5 %collective-permute-start.4 = (f32[8,1024]{1,0:T(8,128)S(1)}, f32[8,1024]{1,0:T(8,128)S(1)}, u32[]{:S(2)}, u32[]{:S(2)}) collective-permute-start(f32[8,1024]{1,0:T(8,128)S(1)} %fusion), channel_id=1, source_target_pairs={{0,8},{4,12},{8,0},{12,4},{16,24},{20,28},{24,16},{28,20},{1,9},{5... | collective-permute-start | bytes 98312 | tf_op jit(solution)/shard_map/ppermute | solution.py:340
  15.9 1.1 %table_one.1 = (bf16[512,2048]{1,0:T(8,128)(2,1)S(1)}, bf16[512,2048]{1,0:T(8,128)(2,1)S(1)}) custom-call(f32[128,32]{1,0:T(8,128)S(1)} %get-tuple-element.24.refs_1_.refs_4_.cols_ref, f32[1,2048]{1,0:T(1,128)S(1)} %get-tuple-element.25.refs_2_.roots_ref), custom_call_target="tpu_custom_call" | custom-call | flops 2097152000 | bytes 421888000 | tf_op jit(solution)/shard_map/table_one/pallas_call | solution.py:287
  17.1 1.3 %collective-permute-done.4 = f32[8,1024]{1,0:T(8,128)S(1)} collective-permute-done((f32[8,1024]{1,0:T(8,128)S(1)}, f32[8,1024]{1,0:T(8,128)S(1)}, u32[]{:S(2)}, u32[]{:S(2)}) %collective-permute-start.4) | collective-permute-done | bytes 32800 | tf_op jit(solution)/shard_map/ppermute | solution.py:340
  18.4 3.6 %norm_one.1.refs_0_ = f32[2,2048]{1,0:T(2,128)S(1)} custom-call(f32[8,1024]{1,0:T(8,128)S(1)} %fusion.2.refs_0_.refs_2_, f32[128,32]{1,0:T(8,128)S(1)} %get-tuple-element.24.refs_1_.refs_4_.cols_ref, f32[1,2048]{1,0:T(1,128)S(1)} %get-tuple-element.25.refs_2_.roots_ref), custom_call_target="tpu_custom_call" | custom-call | flops 2097152000 | bytes 7372800 | tf_op jit(solution)/shard_map/norm_one/pallas_call | solution.py:287
  22.1 1.6 %table_two.1.two_ref = f32[2048,1024]{1,0:T(8,128)S(1)} custom-call(f32[128,32]{1,0:T(8,128)S(1)} %get-tuple-element.27.refs_5_.refs_0_, f32[1,1024]{1,0:T(1,128)S(1)} %get-tuple-element.28.refs_1_), custom_call_target="tpu_custom_call" | custom-call | flops 2097152000 | bytes 840908800 | tf_op jit(solution)/shard_map/table_two/pallas_call | solution.py:287
  24.0 2.4 %scale.1 = (bf16[2048,1024]{1,0:T(8,128)(2,1)S(1)}, bf16[2048,1024]{1,0:T(8,128)(2,1)S(1)}, f32[1,1024]{1,0:T(1,128)S(1)}) custom-call(f32[128,36]{1,0:T(8,128)S(1)} %weights.1, f32[2048,1024]{1,0:T(8,128)S(1)} %table_two.1.two_ref), custom_call_target="tpu_custom_call" | custom-call | flops 20971520 | bytes 16799744 | tf_op jit(solution)/shard_map/scale/pallas_call | solution.py:287
  26.4 3.6 %mid.1.refs_0_ = f32[256,1024]{1,0:T(8,128)S(1)} custom-call(f32[128,36]{1,0:T(8,128)S(1)} %weights.1, bf16[512,2048]{1,0:T(8,128)(2,1)S(1)} %get-tuple-element.32.high_ref, bf16[512,2048]{1,0:T(8,128)(2,1)S(1)} %get-tuple-element.33.low_ref, bf16[2048,1024]{1,0:T(8,128)(2,1)S(1)} %get-tuple-element.40.b_high, bf16[2048,1024]{1,0:T(8,128)(2,1)S(1)} %get-tuple-element.34.b_low), custom_call_target="tpu_custom_call" | custom-call | flops 3221225472 | bytes 13649920 | tf_op jit(solution)/shard_map/mid/pallas_call | solution.py:287
  30.0 0.6 %collective-permute-start.10 = (f32[256,1024]{1,0:T(8,128)S(1)}, f32[256,1024]{1,0:T(8,128)S(1)}, u32[]{:S(2)}, u32[]{:S(2)}) collective-permute-start(f32[256,1024]{1,0:T(8,128)S(1)} %mid.1.refs_0_), channel_id=1, source_target_pairs={{0,4},{4,0},{8,12},{12,8},{16,20},{20,16},{24,28},{28,24},{1,5},{5... | collective-permute-start | bytes 3145736 | tf_op jit(solution)/shard_map/ppermute | solution.py:389
  30.6 4.5 %collective-permute-done.7.refs_3_ = f32[512,256]{1,0:T(8,128)S(1)} collective-permute-done((f32[512,256]{1,0:T(8,128)}, f32[512,256]{1,0:T(8,128)S(1)}, u32[]{:S(2)}, u32[]{:S(2)}) %collective-permute-start.7) | collective-permute-done | bytes 524320 | tf_op jit(solution)/shard_map/ppermute | solution.py:320
  35.1 1.3 %collective-permute-start.8 = (f32[512,256]{1,0:T(8,128)S(1)}, f32[512,256]{1,0:T(8,128)S(1)}, u32[]{:S(2)}, u32[]{:S(2)}) collective-permute-start(f32[512,256]{1,0:T(8,128)S(1)} %collective-permute-done.7.refs_3_), channel_id=1, source_target_pairs={{1,0},{2,3},{5,4},{6,7},{9,8},{10,11},{13,12},{14,15},{17,16},{18,... | collective-permute-start | bytes 1572872 | tf_op jit(solution)/shard_map/ppermute | solution.py:320
  36.4 3.4 %mid_late.1 = (f32[128,1024]{1,0:T(8,128)S(1)}, f32[128,1024]{1,0:T(8,128)S(1)}) custom-call(f32[128,36]{1,0:T(8,128)S(1)} %weights.1, bf16[512,2048]{1,0:T(8,128)(2,1)S(1)} %get-tuple-element.32.high_ref, bf16[512,2048]{1,0:T(8,128)(2,1)S(1)} %get-tuple-element.33.low_ref, bf16[2048,1024]{1,0:T(8,128)(2,1)S(1)} %get-tuple-element.40.b_high, ...), custom_call_target="tpu_custom_call" | custom-call | flops 19327352832 | bytes 81899520 | tf_op jit(solution)/shard_map/mid_late/pallas_call | solution.py:287
  39.9 0.5 %collective-permute-start.13 = (f32[128,1024]{1,0:T(8,128)S(1)}, f32[128,1024]{1,0:T(8,128)S(1)}, u32[]{:S(2)}, u32[]{:S(2)}) collective-permute-start(f32[128,1024]{1,0:T(8,128)S(1)} %get-tuple-element.42.refs_8_), channel_id=1, source_target_pairs={{0,4},{4,0},{8,12},{12,8},{16,20},{20,16},{24,28},{28,24},{1,5},{5... | collective-permute-start | bytes 1572872 | tf_op jit(solution)/shard_map/ppermute | solution.py:389
  40.4 1.5 %collective-permute-start.11 = (f32[1,1024]{1,0:T(1,128)S(1)}, f32[1,1024]{1,0:T(1,128)S(1)}, u32[]{:S(2)}, u32[]{:S(2)}) collective-permute-start(f32[1,1024]{1,0:T(1,128)S(1)} %get-tuple-element.38.refs_4_), channel_id=1, source_target_pairs={{0,16},{4,20},{8,24},{12,28},{16,0},{20,4},{24,8},{28,12},{1,17},{... | collective-permute-start | bytes 12296 | tf_op jit(solution)/shard_map/ppermute | solution.py:376
  41.9 1.8 %apply.1.refs_3_ = f32[512,1024]{1,0:T(8,128)S(1)} custom-call(f32[256,1024]{1,0:T(8,128)S(1)} %mid.1.refs_0_, f32[256,1024]{1,0:T(8,128)S(1)} %collective-permute-done.10.refs_1_, f32[512,256]{1,0:T(8,128)S(1)} %copy-done, f32[512,256]{1,0:T(8,128)S(1)} %collective-permute-done.7.refs_3_), custom_call_target="tpu_custom_call" | custom-call | flops 1610612 | bytes 5242 | tf_op jit(solution)/shard_map/apply/pallas_call | solution.py:287
  43.8 2.7 %collective-permute-done.8.refs_1_ = f32[512,256]{1,0:T(8,128)S(1)} collective-permute-done((f32[512,256]{1,0:T(8,128)S(1)}, f32[512,256]{1,0:T(8,128)S(1)}, u32[]{:S(2)}, u32[]{:S(2)}) %collective-permute-start.8) | collective-permute-done | bytes 524320 | tf_op jit(solution)/shard_map/ppermute | solution.py:320
  46.5 2.8 %finish.1 = f32[512,1024]{1,0:T(8,128)} custom-call(f32[512,256]{1,0:T(8,128)S(1)} %collective-permute-done.6.refs_0_, f32[512,256]{1,0:T(8,128)S(1)} %collective-permute-done.8.refs_1_, f32[512,256]{1,0:T(8,128)S(1)} %collective-permute-done.9.refs_2_, f32[512,1024]{1,0:T(8,128)S(1)} %apply.1.refs_3_, f32[1,1024]{1,0:T(1,128)S(1)} %get-tuple-element.38.refs_4_, ...), custom_call_target="tpu_custom_call" | custom-call | flops 1610612 | bytes 7876 | tf_op jit(solution)/shard_map/finish/pallas_call | solution.py:287
  (26 shorter events, 0.9 us)
Async XLA Ops:
  0.7 10.1 %collective-permute-start = (f32[2,256]{1,0:T(2,128)S(1)}, f32[2,256]{1,0:T(2,128)S(1)}, u32[]{:S(2)}, u32[]{:S(2)}) collective-permute-start(f32[2,256]{1,0:T(2,128)S(1)} %pad_maximum_fusion.1), channel_id=1, source_target_pairs={{0,1},{1,0},{2,3},{3,2},{4,5},{5,4},{6,7},{7,6},{8,9},{9,8},{10,11... | collective-permute-start | bytes 6152 | tf_op jit(solution)/shard_map/ppermute | solution.py:320
  3.8 7.8 %collective-permute-start.1 = (f32[2,256]{1,0:T(2,128)S(1)}, f32[2,256]{1,0:T(2,128)S(1)}, u32[]{:S(2)}, u32[]{:S(2)}) collective-permute-start(f32[2,256]{1,0:T(2,128)S(1)} %pad_maximum_fusion.1), channel_id=1, source_target_pairs={{0,2},{1,3},{2,0},{3,1},{4,6},{5,7},{6,4},{7,5},{8,10},{9,11},{10,... | collective-permute-start | bytes 6152 | tf_op jit(solution)/shard_map/ppermute | solution.py:320
  6.4 5.5 %collective-permute-start.2 = (f32[2,256]{1,0:T(2,128)S(1)}, f32[2,256]{1,0:T(2,128)S(1)}, u32[]{:S(2)}, u32[]{:S(2)}) collective-permute-start(f32[2,256]{1,0:T(2,128)S(1)} %pad_maximum_fusion.1), channel_id=1, source_target_pairs={{0,3},{1,2},{2,1},{3,0},{4,7},{5,6},{6,5},{7,4},{8,11},{9,10},{10,... | collective-permute-start | bytes 6152 | tf_op jit(solution)/shard_map/ppermute | solution.py:320
  6.4 24.2 %collective-permute-start.6 = (f32[512,256]{1,0:T(8,128)}, f32[512,256]{1,0:T(8,128)S(1)}, u32[]{:S(2)}, u32[]{:S(2)}) collective-permute-start(f32[512,256]{1,0:T(8,128)} %refs_2_.3), channel_id=1, source_target_pairs={{0,1},{1,0},{2,3},{3,2},{4,5},{5,4},{6,7},{7,6},{8,9},{9,8},{10,11... | collective-permute-start | bytes 1572872 | tf_op jit(solution)/shard_map/ppermute | solution.py:320
  7.3 27.8 %collective-permute-start.7 = (f32[512,256]{1,0:T(8,128)}, f32[512,256]{1,0:T(8,128)S(1)}, u32[]{:S(2)}, u32[]{:S(2)}) collective-permute-start(f32[512,256]{1,0:T(8,128)} %refs_2_.3), channel_id=1, source_target_pairs={{0,2},{1,3},{2,0},{3,1},{4,6},{5,7},{6,4},{7,5},{8,10},{9,11},{10,... | collective-permute-start | bytes 1572872 | tf_op jit(solution)/shard_map/ppermute | solution.py:320
  10.9 32.9 %collective-permute-start.9 = (f32[512,256]{1,0:T(8,128)}, f32[512,256]{1,0:T(8,128)S(1)}, u32[]{:S(2)}, u32[]{:S(2)}) collective-permute-start(f32[512,256]{1,0:T(8,128)} %refs_2_.3), channel_id=1, source_target_pairs={{1,2},{2,1},{5,6},{6,5},{9,10},{10,9},{13,14},{14,13},{17,18},{18,... | collective-permute-start | bytes 1572872 | tf_op jit(solution)/shard_map/ppermute | solution.py:320
  12.0 2.3 %collective-permute-start.3 = (f32[8,1024]{1,0:T(8,128)S(1)}, f32[8,1024]{1,0:T(8,128)S(1)}, u32[]{:S(2)}, u32[]{:S(2)}) collective-permute-start(f32[8,1024]{1,0:T(8,128)S(1)} %maximum_maximum_fusion), channel_id=1, source_target_pairs={{0,4},{4,0},{8,12},{12,8},{16,20},{20,16},{24,28},{28,24},{1,5},{5... | collective-permute-start | bytes 98312 | tf_op jit(solution)/shard_map/ppermute | solution.py:340
  14.4 3.9 %collective-permute-start.4 = (f32[8,1024]{1,0:T(8,128)S(1)}, f32[8,1024]{1,0:T(8,128)S(1)}, u32[]{:S(2)}, u32[]{:S(2)}) collective-permute-start(f32[8,1024]{1,0:T(8,128)S(1)} %fusion), channel_id=1, source_target_pairs={{0,8},{4,12},{8,0},{12,4},{16,24},{20,28},{24,16},{28,20},{1,9},{5... | collective-permute-start | bytes 98312 | tf_op jit(solution)/shard_map/ppermute | solution.py:340
  22.0 1.6 %collective-permute-start.5 = (f32[2,2048]{1,0:T(2,128)S(1)}, f32[2,2048]{1,0:T(2,128)S(1)}, u32[]{:S(2)}, u32[]{:S(2)}) collective-permute-start(f32[2,2048]{1,0:T(2,128)S(1)} %norm_one.1.refs_0_), channel_id=1, source_target_pairs={{0,4},{4,0},{8,12},{12,8},{16,20},{20,16},{24,28},{28,24},{1,5},{5... | collective-permute-start | bytes 49160 | tf_op jit(solution)/shard_map/ppermute | solution.py:358
  30.0 11.9 %copy-start = (f32[512,256]{1,0:T(8,128)S(1)}, f32[512,256]{1,0:T(8,128)}, u32[]{:S(2)}) copy-start(f32[512,256]{1,0:T(8,128)} %refs_2_.3) | copy-start | bytes 1572868
  30.0 10.4 %collective-permute-start.10 = (f32[256,1024]{1,0:T(8,128)S(1)}, f32[256,1024]{1,0:T(8,128)S(1)}, u32[]{:S(2)}, u32[]{:S(2)}) collective-permute-start(f32[256,1024]{1,0:T(8,128)S(1)} %mid.1.refs_0_), channel_id=1, source_target_pairs={{0,4},{4,0},{8,12},{12,8},{16,20},{20,16},{24,28},{28,24},{1,5},{5... | collective-permute-start | bytes 3145736 | tf_op jit(solution)/shard_map/ppermute | solution.py:389
  35.1 11.4 %collective-permute-start.8 = (f32[512,256]{1,0:T(8,128)S(1)}, f32[512,256]{1,0:T(8,128)S(1)}, u32[]{:S(2)}, u32[]{:S(2)}) collective-permute-start(f32[512,256]{1,0:T(8,128)S(1)} %collective-permute-done.7.refs_3_), channel_id=1, source_target_pairs={{1,0},{2,3},{5,4},{6,7},{9,8},{10,11},{13,12},{14,15},{17,16},{18,... | collective-permute-start | bytes 1572872 | tf_op jit(solution)/shard_map/ppermute | solution.py:320
  39.8 6.6 %collective-permute-start.12 = (f32[128,1024]{1,0:T(8,128)S(1)}, f32[128,1024]{1,0:T(8,128)S(1)}, u32[]{:S(2)}, u32[]{:S(2)}) collective-permute-start(f32[128,1024]{1,0:T(8,128)S(1)} %get-tuple-element.41.refs_7_), channel_id=1, source_target_pairs={{0,4},{4,0},{8,12},{12,8},{16,20},{20,16},{24,28},{28,24},{1,5},{5... | collective-permute-start | bytes 1572872 | tf_op jit(solution)/shard_map/ppermute | solution.py:389
  39.9 6.6 %collective-permute-start.13 = (f32[128,1024]{1,0:T(8,128)S(1)}, f32[128,1024]{1,0:T(8,128)S(1)}, u32[]{:S(2)}, u32[]{:S(2)}) collective-permute-start(f32[128,1024]{1,0:T(8,128)S(1)} %get-tuple-element.42.refs_8_), channel_id=1, source_target_pairs={{0,4},{4,0},{8,12},{12,8},{16,20},{20,16},{24,28},{28,24},{1,5},{5... | collective-permute-start | bytes 1572872 | tf_op jit(solution)/shard_map/ppermute | solution.py:389
  40.4 6.1 %collective-permute-start.11 = (f32[1,1024]{1,0:T(1,128)S(1)}, f32[1,1024]{1,0:T(1,128)S(1)}, u32[]{:S(2)}, u32[]{:S(2)}) collective-permute-start(f32[1,1024]{1,0:T(1,128)S(1)} %get-tuple-element.38.refs_4_), channel_id=1, source_target_pairs={{0,16},{4,20},{8,24},{12,28},{16,0},{20,4},{24,8},{28,12},{1,17},{... | collective-permute-start | bytes 12296 | tf_op jit(solution)/shard_map/ppermute | solution.py:376
